TPU v7x, 256 devices: a whole 4x4x8 slice. The times are simulated.
256 devices in a mesh: dp: 8 (over z_hi, core), seq: 32 (over z_lo, y, x).
Axes of the slice: x: 4, y: 4, z: 8 (z_hi: 4, z_lo: 2; z = z_hi * 2 + z_lo), core: 2. Of those that a mesh axis runs over, the one named last changes fastest.
Arguments:
- tokens: bfloat16 [8, 64, 64, 1152], P('dp', 'seq'), may hold values from -24 to 24
- cotangent: bfloat16 [8, 64, 64, 1152], P('dp', 'seq'), may hold values from -6 to 6
- w_qkv: bfloat16 [1152, 1728], replicated, may hold values from -5 to 5
- w_out: bfloat16 [576, 1152], replicated, may hold values from -0.25 to 0.25
Outputs:
- result: bfloat16 [8, 64, 64, 1152], P('dp', 'seq')
- grad_tokens: bfloat16 [8, 64, 64, 1152], P('dp', 'seq')
- grad_w_qkv: float32 [1152, 1728], P('seq', 'dp')
- grad_w_out: float32 [576, 1152], P('seq', 'dp')
All inputs are finite; a program needn't handle non-finite values.
Results may differ from a plain program's by a relative error of at most 0.034.
Values may be sent and summed in bfloat16 or wider, within the bound.
A program may use at most 64 MiB of HBM per device.

v0:
```python
import jax
import jax.numpy as jnp
from jax import lax
from jax.sharding import PartitionSpec as P

HEADS = 8
HS = 72


epsilon = 1e-06


def normalize(values):
    widened = values.astype(jnp.float32)
    centered = widened - jnp.mean(widened, axis=-1, keepdims=True)
    inv_std = lax.rsqrt(jnp.mean(centered * centered, axis=-1, keepdims=True) + epsilon)
    return (centered * inv_std, inv_std)


def norm_backward(grad_in, x_hat, inv_std):
    first = jnp.mean(grad_in, axis=-1, keepdims=True)
    second = jnp.mean(grad_in * x_hat, axis=-1, keepdims=True)
    return (grad_in - first - x_hat * second) * inv_std


def split_heads(block):
    return block.reshape(block.shape[:-1] + (HEADS, HS))


def join_heads(block):
    return block.reshape(block.shape[:-2] + (HEADS * HS,))


def attend_forward(query_heads, key_heads, value_heads, softmax_scale):
    scores = (
        jnp.einsum("cfphe,cgphe->cphfg", query_heads, key_heads, preferred_element_type=jnp.float32)
        * softmax_scale
    )
    top = jnp.max(scores, axis=-1, keepdims=True)
    expo = jnp.exp(scores - top)
    probs = expo / jnp.sum(expo, axis=-1, keepdims=True)
    probs_low = probs.astype(jnp.bfloat16)
    attended = jnp.einsum(
        "cphfg,cgphe->cfphe", probs_low, value_heads, preferred_element_type=jnp.float32
    ).astype(jnp.bfloat16)
    return (attended, probs, probs_low)


def attend_backward(
    query_heads, key_heads, value_heads, probs, probs_low, grad_heads, softmax_scale
):
    grad_probs = jnp.einsum(
        "cfphe,cgphe->cphfg", grad_heads, value_heads, preferred_element_type=jnp.float32
    )
    delta = jnp.sum(probs * grad_probs, axis=-1, keepdims=True)
    grad_scores = (probs * (grad_probs - delta) * softmax_scale).astype(jnp.bfloat16)
    grad_query = jnp.einsum(
        "cphfg,cgphe->cfphe", grad_scores, key_heads, preferred_element_type=jnp.float32
    ).astype(jnp.bfloat16)
    grad_key = jnp.einsum(
        "cphfg,cfphe->cgphe", grad_scores, query_heads, preferred_element_type=jnp.float32
    ).astype(jnp.bfloat16)
    grad_value = jnp.einsum(
        "cphfg,cfphe->cgphe", probs_low, grad_heads, preferred_element_type=jnp.float32
    ).astype(jnp.bfloat16)
    return (join_heads(grad_query), join_heads(grad_key), join_heads(grad_value))


def project(normed, w_qkv, inner_width):
    flat_normed = normed.reshape(-1, normed.shape[-1])
    projected = jnp.dot(flat_normed, w_qkv, preferred_element_type=jnp.float32).astype(jnp.bfloat16)
    projected = projected.reshape(normed.shape[:3] + (3 * inner_width,))
    return (flat_normed, projected)


def input_grads(grad_query, grad_key, grad_value, flat_normed, w_qkv, x_hat, inv_std):
    grad_proj = jnp.concatenate([grad_query, grad_key, grad_value], axis=-1).reshape(
        flat_normed.shape[0], -1
    )
    grad_w_qkv = lax.dot_general(
        flat_normed, grad_proj, (((0,), (0,)), ((), ())), preferred_element_type=jnp.float32
    )
    grad_normed = lax.dot_general(
        grad_proj, w_qkv, (((1,), (1,)), ((), ())), preferred_element_type=jnp.float32
    )
    grad_branch = norm_backward(grad_normed.reshape(x_hat.shape), x_hat, inv_std).astype(
        jnp.bfloat16
    )
    return (grad_w_qkv, grad_branch)


def shards(tokens, cotangent, w_qkv, w_out):
    clip_count, frame_local, pos_count, width = tokens.shape
    inner_width = w_out.shape[0]
    softmax_scale = HS ** (-0.5)
    x_hat, inv_std = normalize(tokens)
    flat_normed, projected = project(x_hat.astype(jnp.bfloat16), w_qkv, inner_width)
    query_rows, key_rows, value_rows = (
        lax.all_to_all(
            projected[..., :inner_width], "seq", split_axis=2, concat_axis=1, tiled=True
        ),
        lax.all_to_all(
            projected[..., inner_width : 2 * inner_width],
            "seq",
            split_axis=2,
            concat_axis=1,
            tiled=True,
        ),
        lax.all_to_all(
            projected[..., 2 * inner_width :], "seq", split_axis=2, concat_axis=1, tiled=True
        ),
    )
    query_heads = split_heads(query_rows)
    key_heads = split_heads(key_rows)
    value_heads = split_heads(value_rows)
    attended, probs, probs_low = attend_forward(query_heads, key_heads, value_heads, softmax_scale)
    outputs_frames = lax.all_to_all(
        join_heads(attended), "seq", split_axis=1, concat_axis=2, tiled=True
    )
    flat_out = outputs_frames.reshape(-1, inner_width)
    flat_grad = cotangent.reshape(-1, width)
    branch = jnp.dot(flat_out, w_out, preferred_element_type=jnp.float32).reshape(tokens.shape)
    result = (tokens.astype(jnp.float32) + branch).astype(jnp.bfloat16)
    grad_attended = lax.dot_general(
        flat_grad, w_out, (((1,), (1,)), ((), ())), preferred_element_type=jnp.float32
    ).astype(jnp.bfloat16)
    grad_w_out = lax.dot_general(
        flat_out, flat_grad, (((0,), (0,)), ((), ())), preferred_element_type=jnp.float32
    )
    grad_moved = lax.all_to_all(
        grad_attended.reshape(outputs_frames.shape), "seq", split_axis=2, concat_axis=1, tiled=True
    )
    grad_query, grad_key, grad_value = attend_backward(
        query_heads,
        key_heads,
        value_heads,
        probs,
        probs_low,
        split_heads(grad_moved),
        softmax_scale,
    )
    grad_query, grad_key, grad_value = (
        lax.all_to_all(grad_query, "seq", split_axis=1, concat_axis=2, tiled=True),
        lax.all_to_all(grad_key, "seq", split_axis=1, concat_axis=2, tiled=True),
        lax.all_to_all(grad_value, "seq", split_axis=1, concat_axis=2, tiled=True),
    )
    grad_w_qkv, grad_branch = input_grads(
        grad_query, grad_key, grad_value, flat_normed, w_qkv, x_hat, inv_std
    )
    grad_branch = lax.optimization_barrier(grad_branch)
    grad_tokens = (cotangent.astype(jnp.float32) + grad_branch.astype(jnp.float32)).astype(
        jnp.bfloat16
    )
    grad_w_qkv, grad_w_out = (
        lax.psum_scatter(
            grad_w_qkv.astype(jnp.bfloat16), "seq", scatter_dimension=0, tiled=True
        ).astype(jnp.float32),
        lax.psum_scatter(
            grad_w_out.astype(jnp.bfloat16), "seq", scatter_dimension=0, tiled=True
        ).astype(jnp.float32),
    )
    grad_w_qkv, grad_w_out = (
        lax.psum_scatter(
            grad_w_qkv.astype(jnp.bfloat16), "dp", scatter_dimension=1, tiled=True
        ).astype(jnp.float32),
        lax.psum_scatter(
            grad_w_out.astype(jnp.bfloat16), "dp", scatter_dimension=1, tiled=True
        ).astype(jnp.float32),
    )
    token_total = clip_count * lax.axis_size("dp") * frame_local * lax.axis_size("seq") * pos_count
    factor = token_total ** (-0.5)
    return (result, grad_tokens, grad_w_qkv * factor, grad_w_out * factor)


def solution(mesh):
    in_specs = (P("dp", "seq", None, None), P("dp", "seq", None, None), P(), P())
    out_specs = (
        P("dp", "seq", None, None),
        P("dp", "seq", None, None),
        P("seq", "dp"),
        P("seq", "dp"),
    )
    return jax.shard_map(shards, mesh=mesh, in_specs=in_specs, out_specs=out_specs, check_vma=False)
```

profile of v0, /device:TPU:1, one launch (start us, length us, event | category | flops | bytes accessed | tf_op | source)
XLA Modules:
  0.0 670.9 jit_solution(13173540842376963425)
XLA Ops:
  7.2 1.3 copy-done
  8.5 1.5 convolution_convert_fusion.6
  10.1 0.8 copy.61
  11.0 9.2 %all-to-all-start.4 = ((bf16[1,2,64,576]{3,1,0,2:T(2,128)(2,1)}), bf16[1,2,64,576]{3,1,0,2:T(2,128)(2,1)S(1)}, u32[]{:S(2)}, u32[]{:S(2)}) async-start(bf16[1,2,64,576]{3,1,0,2:T(2,128)(2,1)} %copy.61), calls=%async_computation.4 | async-start | bytes 327680 | tf_op jit(solution)/shard_map/all_to_all | solution.py:130
  20.2 1.1 convert_reduce_fusion
  21.3 1.2 fusion.30
  22.5 1.2 fusion.25
  23.7 3.3 convolution_convert_fusion.1
  27.3 0.8 copy.49
  28.2 7.8 %all-to-all-start.1 = ((bf16[1,2,64,576]{3,1,0,2:T(2,128)(2,1)}), bf16[1,2,64,576]{3,1,0,2:T(2,128)(2,1)S(1)}, u32[]{:S(2)}, u32[]{:S(2)}) async-start(bf16[1,2,64,576]{3,1,0,2:T(2,128)(2,1)} %copy.49), calls=%async_computation.1 | async-start | bytes 327680 | tf_op jit(solution)/shard_map/all_to_all | solution.py:99
  35.9 0.8 copy.51
  36.8 6.7 all-to-all-done.1
  43.5 3.9 all-to-all-start.2
  47.3 0.8 copy.47
  48.2 6.7 %all-to-all-done.2 = bf16[1,2,64,576]{3,1,0,2:T(2,128)(2,1)S(1)} async-done(((bf16[1,2,64,576]{3,1,0,2:T(2,128)(2,1)}), bf16[1,2,64,576]{3,1,0,2:T(2,128)(2,1)S(1)}, u32[]{:S(2)}, u32[]{:S(2)}) %all-to-all-start.2) | async-done | bytes 147488 | tf_op jit(solution)/shard_map/all_to_all | solution.py:102
  54.9 3.9 all-to-all-start
  58.9 0.3 reshape.202
  59.3 0.3 reshape.196
  59.7 0.3 reshape.197
  60.0 6.2 all-to-all-done
  66.4 0.3 reshape.195
  66.7 1.1 fusion.62
  67.8 1.3 fusion.13
  69.3 1.2 reshape.212
  70.5 3.9 all-to-all-start.3
  74.6 1.6 fusion.14
  76.4 1.2 reshape.213
  77.6 4.2 all-to-all-done.3
  81.8 3.9 all-to-all-start.5
  85.7 1.5 fusion.15
  87.4 1.2 reshape.214
  88.6 4.6 all-to-all-done.5
  93.2 4.0 all-to-all-start.6
  97.3 1.3 fusion.16
  98.7 1.2 reshape.215
  99.9 4.7 all-to-all-done.6
  104.6 3.9 all-to-all-start.7
  108.5 0.6 dynamic-slice.2
  109.8 0.6 fusion.61
  112.3 0.8 concatenate.12
  113.5 2.5 all-to-all-done.7
  116.2 0.8 concatenate.14
  117.2 3.2 fusion.3
  120.4 86.5 %fusion = bf16[40,1728]{1,0:T(8,128)(2,1)} fusion(bf16[1152,1728]{1,0:T(8,128)(2,1)} %fusion.3), kind=kCustom, calls=%all-reduce-scatter | all-reduce-scatter fusion | flops 2211841 | bytes 4120576
  206.9 0.8 slice.15
  207.7 1.3 collective-permute-start.2
  209.0 2.0 collective-permute-start.1
  210.9 1.9 collective-permute-start
  213.1 3.0 fusion.67
  216.4 1.6 convolution_convert_fusion
  218.1 0.3 fusion.29
  218.4 1.3 collective-permute-start.3
  219.7 0.8 add_convert_fusion
  220.5 1.1 fusion.5
  221.6 3.4 concatenate.17
  225.0 0.7 constant_dynamic-slice_fusion
  225.7 308.3 %all-reduce.9.cloned.1.call-done = bf16[576,1152]{1,0:T(8,128)(2,1)} async-done(((bf16[576,1152]{1,0:T(8,128)(2,1)}), bf16[576,1152]{1,0:T(8,128)(2,1)}) %all-reduce.9.cloned.1.call-update) | async-done | bytes 1327120
  534.0 0.9 constant_dynamic-slice_fusion.1
  534.9 0.9 copy.90
  535.9 91.4 %all-reduce.7.cloned.1.call-done = bf16[36,1728]{1,0:T(8,128)(2,1)} async-done(((bf16[36,1728]{1,0:T(8,128)(2,1)}), bf16[36,1728]{1,0:T(8,128)(2,1)}) %all-reduce.7.cloned.1.call-update) | async-done | bytes 124432
  627.3 1.4 convert_multiply_fusion
  628.8 34.1 %reduce-scatter.7.cloned.1.call-done = bf16[144,18]{1,0:T(8,128)(2,1)} async-done(((bf16[1152,18]{1,0:T(8,128)(2,1)}), bf16[144,18]{1,0:T(8,128)(2,1)}) %reduce-scatter.7.cloned.1.call-update) | async-done | bytes 5200
  662.9 0.8 copy.91
  663.7 0.6 convert_multiply_fusion.1
  (56 shorter events, 4.1 us)
Async XLA Ops:
  7.2 1.3 copy-start
  11.0 17.2 %all-to-all-start.4 = ((bf16[1,2,64,576]{3,1,0,2:T(2,128)(2,1)}), bf16[1,2,64,576]{3,1,0,2:T(2,128)(2,1)S(1)}, u32[]{:S(2)}, u32[]{:S(2)}) async-start(bf16[1,2,64,576]{3,1,0,2:T(2,128)(2,1)} %copy.61), calls=%async_computation.4 | async-start | bytes 327680 | tf_op jit(solution)/shard_map/all_to_all | solution.py:130
  28.2 15.3 %all-to-all-start.1 = ((bf16[1,2,64,576]{3,1,0,2:T(2,128)(2,1)}), bf16[1,2,64,576]{3,1,0,2:T(2,128)(2,1)S(1)}, u32[]{:S(2)}, u32[]{:S(2)}) async-start(bf16[1,2,64,576]{3,1,0,2:T(2,128)(2,1)} %copy.49), calls=%async_computation.1 | async-start | bytes 327680 | tf_op jit(solution)/shard_map/all_to_all | solution.py:99
  43.5 11.4 %all-to-all-start.2 = ((bf16[1,2,64,576]{3,1,0,2:T(2,128)(2,1)}), bf16[1,2,64,576]{3,1,0,2:T(2,128)(2,1)S(1)}, u32[]{:S(2)}, u32[]{:S(2)}) async-start(bf16[1,2,64,576]{3,1,0,2:T(2,128)(2,1)} %copy.51), calls=%async_computation.2 | async-start | bytes 327680 | tf_op jit(solution)/shard_map/all_to_all | solution.py:102
  54.9 11.4 %all-to-all-start = ((bf16[1,2,64,576]{3,1,0,2:T(2,128)(2,1)}), bf16[1,2,64,576]{3,1,0,2:T(2,128)(2,1)S(1)}, u32[]{:S(2)}, u32[]{:S(2)}) async-start(bf16[1,2,64,576]{3,1,0,2:T(2,128)(2,1)} %copy.47), calls=%async_computation | async-start | bytes 327680 | tf_op jit(solution)/shard_map/all_to_all | solution.py:109
  60.0 10.5 %copy-start.5 = (bf16[64,2,8,72]{3,2,1,0:T(8,128)(2,1)}, bf16[64,2,8,72]{3,2,1,0:T(8,128)(2,1)S(1)}, u32[]{:S(2)}) copy-start(bf16[64,2,8,72]{3,2,1,0:T(8,128)(2,1)S(1)} %reshape.197) | copy-start | bytes 442372
  70.5 11.4 %all-to-all-start.3 = ((bf16[1,64,2,576]{3,2,0,1:T(2,128)(2,1)}), bf16[1,64,2,576]{3,2,0,1:T(2,128)(2,1)S(1)}, u32[]{:S(2)}, u32[]{:S(2)}) async-start(bf16[1,64,2,576]{3,2,0,1:T(2,128)(2,1)} %reshape.212), calls=%async_computation.3 | async-start | bytes 327680 | tf_op jit(solution)/shard_map/all_to_all | solution.py:117
  77.6 30.9 %copy-start.7 = (u32[256]{0:T(256)S(1)}, u32[256]{0:T(256)}, u32[]{:S(2)}) copy-start(u32[256]{0:T(256)} %constant.25) | copy-start | bytes 3076
  77.6 32.2 %copy-start.6 = (u32[256]{0:T(256)S(1)}, u32[256]{0:T(256)}, u32[]{:S(2)}) copy-start(u32[256]{0:T(256)} %constant.21) | copy-start | bytes 3076
  81.8 11.4 %all-to-all-start.5 = ((bf16[1,64,2,576]{3,2,0,1:T(2,128)(2,1)}), bf16[1,64,2,576]{3,2,0,1:T(2,128)(2,1)S(1)}, u32[]{:S(2)}, u32[]{:S(2)}) async-start(bf16[1,64,2,576]{3,2,0,1:T(2,128)(2,1)} %reshape.213), calls=%async_computation.5 | async-start | bytes 327680 | tf_op jit(solution)/shard_map/all_to_all | solution.py:143
  93.2 11.4 %all-to-all-start.6 = ((bf16[1,64,2,576]{3,2,0,1:T(2,128)(2,1)}), bf16[1,64,2,576]{3,2,0,1:T(2,128)(2,1)S(1)}, u32[]{:S(2)}, u32[]{:S(2)}) async-start(bf16[1,64,2,576]{3,2,0,1:T(2,128)(2,1)} %reshape.214), calls=%async_computation.6 | async-start | bytes 327680 | tf_op jit(solution)/shard_map/all_to_all | solution.py:144
  104.6 11.4 %all-to-all-start.7 = ((bf16[1,64,2,576]{3,2,0,1:T(2,128)(2,1)}), bf16[1,64,2,576]{3,2,0,1:T(2,128)(2,1)S(1)}, u32[]{:S(2)}, u32[]{:S(2)}) async-start(bf16[1,64,2,576]{3,2,0,1:T(2,128)(2,1)} %reshape.215), calls=%async_computation.7 | async-start | bytes 327680 | tf_op jit(solution)/shard_map/all_to_all | solution.py:145
  108.5 425.6 %all-reduce.9.cloned.1.call-start = ((), (), s32[]{:S(2)}) async-start(), calls=%async_computation.11 | async-start | bytes 2654208
  120.4 92.5 %copy-start.3 = (bf16[128,576]{1,0:T(8,128)(2,1)S(1)}, bf16[128,576]{1,0:T(8,128)(2,1)}, u32[]{:S(2)}) copy-start(bf16[128,576]{1,0:T(8,128)(2,1)} %concatenate.12) | copy-start | bytes 442372
  120.4 92.5 %copy-start.4 = (bf16[128,576]{1,0:T(8,128)(2,1)S(1)}, bf16[128,576]{1,0:T(8,128)(2,1)}, u32[]{:S(2)}) copy-start(bf16[128,576]{1,0:T(8,128)(2,1)} %concatenate.14) | copy-start | bytes 442372
  206.9 9.3 %copy-start.1 = (bf16[1,2,64,1152]{3,2,1,0:T(8,128)(2,1)S(1)}, bf16[1,2,64,1152]{3,2,1,0:T(8,128)(2,1)}, u32[]{:S(2)}) copy-start(bf16[1,2,64,1152]{3,2,1,0:T(8,128)(2,1)} %param.4) | copy-start | bytes 884740
  206.9 9.5 %copy-start.2 = (bf16[1,2,64,1152]{3,2,1,0:T(8,128)(2,1)S(1)}, bf16[1,2,64,1152]{3,2,1,0:T(8,128)(2,1)}, u32[]{:S(2)}) copy-start(bf16[1,2,64,1152]{3,2,1,0:T(8,128)(2,1)} %param.5) | copy-start | bytes 884740
  207.7 13.9 %collective-permute-start.2 = (bf16[40,1728]{1,0:T(8,128)(2,1)}, bf16[40,1728]{1,0:T(8,128)(2,1)S(1)}, u32[]{:S(2)}, u32[]{:S(2)}) collective-permute-start(bf16[40,1728]{1,0:T(8,128)(2,1)} %fusion), channel_id=1, source_target_pairs={{0,3},{1,4},{2,5},{3,6},{4,7},{5,8},{6,9},{7,10},{8,11},{9,12},{10... | collective-permute-start | bytes 414728
  209.0 12.6 %collective-permute-start.1 = (bf16[40,1728]{1,0:T(8,128)(2,1)}, bf16[40,1728]{1,0:T(8,128)(2,1)}, u32[]{:S(2)}, u32[]{:S(2)}) collective-permute-start(bf16[40,1728]{1,0:T(8,128)(2,1)} %fusion), channel_id=1, source_target_pairs={{0,2},{1,3},{2,4},{3,5},{4,6},{5,7},{6,8},{7,9},{8,10},{9,11},{10,... | collective-permute-start | bytes 414728
  210.9 10.6 %collective-permute-start = (bf16[40,1728]{1,0:T(8,128)(2,1)}, bf16[40,1728]{1,0:T(8,128)(2,1)}, u32[]{:S(2)}, u32[]{:S(2)}) collective-permute-start(bf16[40,1728]{1,0:T(8,128)(2,1)} %fusion), channel_id=1, source_target_pairs={{0,1},{1,2},{2,3},{3,4},{4,5},{5,6},{6,7},{7,8},{8,9},{9,10},{10,1... | collective-permute-start | bytes 414728
  218.0 409.3 %all-reduce.7.cloned.1.call-start = ((), (), s32[]{:S(2)}) async-start(), calls=%async_computation.10 | async-start | bytes 286720
  218.4 3.2 collective-permute-start.3
  225.7 437.2 %reduce-scatter.7.cloned.1.call-start = ((), (), s32[]{:S(2)}) async-start(), calls=%async_computation.9 | async-start | bytes 331776
Sparse Core Ops, SparseCore 0:
  218.2 315.8 all-reduce.8
  536.8 90.4 all-reduce.6
  629.8 33.0 reduce-scatter.6
where the time goes:
time: 673 us; the launch traced here: 671 us
  waiting for transfers between devices  470 us (70%)
  blocking collectives  86.5 us (13%)
  starting transfers between devices  46.9 us (7%)
  local copies, waits for them, and re-layouts  24.1 us (4%)
  matrix products  20.8 us (3%)
  between operations  16.1 us (2%)
  other arithmetic  6.86 us (1%)
    unnamed x10, waiting for transfers between devices  434 us
    unnamed x1, blocking collectives  86.5 us
  transfers between devices with their start and end apart: 15, of which 10 were waited for; matrix products, arithmetic and copies ran while one was open for 5% of the time, Pallas kernels for 0%

commit v1 on v0

v1 whole, which is shorter than its diff:
```python
import functools

import jax
import jax.numpy as jnp
from jax import lax
from jax.experimental import pallas as pl
from jax.experimental.pallas import tpu as pltpu
from jax.sharding import PartitionSpec as P

MESH = pl.DeviceIdType.MESH
F32, BF16 = jnp.float32, jnp.bfloat16

D = 1152
HEADS = 8
HS = 72
HD = 576
ROWS = 128
SEQ = 32
PLANE = 16
EPS = 1e-6
SCALE = HS ** (-0.5)
FACTOR = 32768 ** (-0.5)


def dot(a, b, contract):
    return lax.dot_general(a, b, ((contract[:1], contract[1:]), ((), ())), preferred_element_type=F32)


def kernel(
    tok, cot, wqkv_hbm, wout_hbm,
    result, gtok, gwq, gwo,
    wqkv, wout,
    wide, slim, xhat, cotp,
    xs, xr, gs, gr, ats, atr, gbs, gbr,
    cotq, cotr, ntr, arr, amine, apart, gph, gpart, tmine, tpart,
    qb, kb, vb, gab, probs, plow,
    dsend, drecv, dsum, zsend, zrecv, wsend, wrecv, wsum, vsend, vrecv,
    wsem, x_ss, x_rs, g_ss, g_rs, at_ss, at_rs, gb_ss, gb_rs, c_ss, c_rs,
    d_ss, d_rs, z_ss, z_rs, w_ss, w_rs, v_ss, v_rs,
):
    dp, seq = lax.axis_index("dp"), lax.axis_index("seq")
    core, z_hi = dp % 2, dp // 2
    xy, z_lo = seq % PLANE, seq // PLANE
    mate = z_hi * 2 + 1 - core
    zed = z_hi * 2 + z_lo

    def remote(src, dst, send_sem, recv_sem, to_dp, to_seq):
        return pltpu.make_async_remote_copy(
            src_ref=src, dst_ref=dst, send_sem=send_sem, recv_sem=recv_sem,
            device_id=(to_dp, to_seq), device_id_type=MESH,
        )

    barrier = pltpu.get_barrier_semaphore()

    def greet(to_dp, to_seq):
        pl.semaphore_signal(barrier, inc=1, device_id=(to_dp, to_seq), device_id_type=MESH)

    @pl.loop(1, SEQ)
    def _(k):
        greet(dp, (seq + k) % SEQ)

    @pl.loop(1, 8)
    def _(k):
        greet((dp + k) % 8, xy)
        greet((dp + k) % 8, PLANE + xy)

    @pl.loop(1, PLANE)
    def _(k):
        greet(mate, z_lo * PLANE + (xy + k) % PLANE)

    load_wqkv = pltpu.make_async_copy(wqkv_hbm, wqkv, wsem.at[0])
    load_wout = pltpu.make_async_copy(wout_hbm, wout, wsem.at[1])
    load_wout.start()
    load_wqkv.start()

    new = lax.broadcasted_iota(jnp.int32, (ROWS, ROWS), 0)
    old = lax.broadcasted_iota(jnp.int32, (ROWS, ROWS), 1)
    place = ((new >> 1) & 1) * 64 + (new >> 2) * 2 + (new & 1)
    move = jnp.where(place == old, 1.0, 0.0).astype(BF16)

    def pack(rows, block):
        for p in range(SEQ):
            block[p] = rows[4 * p : 4 * p + 4, :].astype(BF16)

    def unpack(block, rows):
        for p in range(SEQ):
            rows[4 * p : 4 * p + 4, :] = block[p].astype(F32)

    def push_all(src, dst, ss, rs):
        @pl.loop(1, SEQ)
        def _(k):
            to = (seq + k) % SEQ
            remote(src.at[to], dst.at[seq], ss.at[to], rs.at[seq], dp, to).start()

        dst[seq] = src[seq]

    def take_all(src, dst, ss, rs):
        @pl.loop(1, SEQ)
        def _(k):
            come = (seq + k) % SEQ
            remote(src.at[come], dst.at[come], ss.at[come], rs.at[come], dp, come).wait_recv()

    def sent_all(src, dst, ss, rs):
        @pl.loop(1, SEQ)
        def _(k):
            to = (seq + k) % SEQ
            remote(src.at[to], dst.at[to], ss.at[to], rs.at[to], dp, to).wait_send()

    wide[...] = dot(move, tok[...], (1, 0))
    pack(wide, xs)
    pl.semaphore_wait(barrier, SEQ - 1 + 14 + PLANE - 1)
    push_all(xs, xr, x_ss, x_rs)

    cotp[...] = dot(move, cot[...], (1, 0)).astype(BF16)
    load_wout.wait()
    slim[...] = dot(cotp[...], wout[...], (1, 1))
    pack(slim, gs)
    push_all(gs, gr, g_ss, g_rs)
    for q in range(4):
        cotq[q] = cotp[:, 288 * q : 288 * q + 288]
    swap_cot = remote(cotq.at[pl.ds(2 * (1 - core), 2)], cotr, c_ss.at[0], c_rs.at[0], mate, seq)
    swap_cot.start()

    take_all(xs, xr, x_ss, x_rs)
    unpack(xr, wide)
    x = wide[...]
    centered = x - jnp.mean(x, axis=-1, keepdims=True)
    inv_std = lax.rsqrt(jnp.mean(centered * centered, axis=-1, keepdims=True) + EPS)
    x_hat = centered * inv_std
    xhat[...] = x_hat
    load_wqkv.wait()
    projected = dot(x_hat.astype(BF16), wqkv[...], (1, 0))
    query = projected[:, :HD].astype(BF16)
    key = projected[:, HD : 2 * HD].astype(BF16)
    value = projected[:, 2 * HD :].astype(BF16)
    lane = lax.broadcasted_iota(jnp.int32, (ROWS, HD), 1)

    def stack(block, out):
        wide_block = block.astype(F32)
        for h in range(HEADS):
            inside = (lane >= h * HS) & (lane < (h + 1) * HS)
            out[h * ROWS : (h + 1) * ROWS, :] = jnp.where(inside, wide_block, 0.0).astype(BF16)

    def side(block):
        return jnp.concatenate([block[h * ROWS : (h + 1) * ROWS, :] for h in range(HEADS)], axis=1)

    stack(query, qb)
    stack(value, vb)
    scores = dot(qb[...], key, (1, 1)) * SCALE
    here = lax.broadcasted_iota(jnp.int32, (HEADS * ROWS, ROWS), 0)
    there = lax.broadcasted_iota(jnp.int32, (HEADS * ROWS, ROWS), 1)
    scores = jnp.where(((here ^ there) & 1) == 0, scores, -jnp.inf)
    expo = jnp.exp(scores - jnp.max(scores, axis=-1, keepdims=True))
    prob = expo / jnp.sum(expo, axis=-1, keepdims=True)
    probs[...] = prob
    plow[...] = prob.astype(BF16)
    slim[...] = dot(side(plow), vb[...], (1, 0))
    pack(slim, ats)
    push_all(ats, atr, at_ss, at_rs)

    ntr[...] = xhat[...].T
    for p in range(PLANE):
        arr[80 * p : 80 * p + 36, :] = ntr[36 * p : 36 * p + 36, :]
        arr[80 * p + 36 : 80 * p + 72, :] = ntr[36 * (PLANE + p) : 36 * (PLANE + p) + 36, :]
        arr[80 * p + 72 : 80 * p + 80, :] = jnp.zeros((8, ROWS), F32)
    amine[...] = arr[...].astype(BF16)
    swap_a = remote(amine, apart, c_ss.at[1], c_rs.at[1], mate, seq)
    swap_a.start()

    stack(key, kb)
    take_all(gs, gr, g_ss, g_rs)
    unpack(gr, slim)
    stack(slim[...], gab)
    grad_probs = dot(gab[...], value, (1, 1))
    prob = probs[...]
    delta = jnp.sum(prob * grad_probs, axis=-1, keepdims=True)
    grad_scores = (prob * (grad_probs - delta) * SCALE).astype(BF16)
    grad_query = dot(side(grad_scores), kb[...], (1, 0))
    grad_key = dot(grad_scores, qb[...], (0, 0))
    grad_value = dot(plow[...], gab[...], (0, 0))
    grad_proj = jnp.concatenate([grad_query, grad_key, grad_value], axis=1)
    gph[0] = grad_proj[:, :864].astype(BF16)
    gph[1] = grad_proj[:, 864:].astype(BF16)
    swap_g = remote(gph.at[1 - core], gpart, c_ss.at[2], c_rs.at[2], mate, seq)
    swap_g.start()
    grad_proj = grad_proj.astype(BF16)

    swap_a.wait_recv()
    swap_g.wait_recv()
    right = jnp.concatenate([gph[core], gpart[...]], axis=0)

    def plane_copy(k):
        to = (xy + k) % PLANE
        return remote(
            dsend.at[to], drecv.at[xy], d_ss.at[to], d_rs.at[xy], dp, z_lo * PLANE + to
        )

    @pl.loop(1, PLANE + 1)
    def _(k):
        to = (xy + k) % PLANE
        rows = pl.ds(pl.multiple_of(to * 80, 16), 80)
        left = jnp.concatenate([amine[rows, :], apart[rows, :]], axis=1)
        dsend[to] = dot(left, right, (1, 0)).astype(BF16)

        @pl.when(k < PLANE)
        def _():
            plane_copy(k).start()

    grad_normed = dot(grad_proj, wqkv[...], (1, 1))
    x_hat = xhat[...]
    first = jnp.mean(grad_normed, axis=-1, keepdims=True)
    second = jnp.mean(grad_normed * x_hat, axis=-1, keepdims=True)
    wide[...] = (grad_normed - first - x_hat * second) * inv_std
    pack(wide, gbs)
    push_all(gbs, gbr, gb_ss, gb_rs)

    take_all(ats, atr, at_ss, at_rs)
    unpack(atr, slim)
    back = slim[...].astype(BF16)
    tmine[...] = slim[...].T.astype(BF16)
    swap_t = remote(tmine, tpart, c_ss.at[3], c_rs.at[3], mate, seq)
    swap_t.start()
    ordered = dot(move, back, (0, 0)).astype(BF16)
    branch = dot(ordered, wout[...], (1, 0))
    result[...] = (tok[...].astype(F32) + branch).astype(BF16)
    swap_cot.wait_recv()
    swap_t.wait_recv()

    def z_target(n):
        return 4 * core + n // 2, (n % 2) * PLANE + xy

    for j in range(2):
        right = jnp.concatenate([cotq[2 * core + j], cotr[j]], axis=0)
        left = jnp.concatenate([tmine[...], tpart[...]], axis=1)
        product = dot(left, right, (1, 0))
        for c in range(2):
            for half in range(2):
                n = (2 * j + c) * 2 + half
                begin = half * 288 + c * 144
                wsend[n] = product[begin : begin + 144, :].astype(BF16)

    def z_push(src, dst, ss, rs):
        @pl.loop(0, 8)
        def _(n):
            to_dp, to_seq = z_target(n)
            own = (to_dp == dp) & (to_seq == seq)

            @pl.when(own)
            def _():
                dst[zed] = src[n]

            @pl.when(jnp.logical_not(own))
            def _():
                remote(src.at[n], dst.at[zed], ss.at[n], rs.at[zed], to_dp, to_seq).start()

    def z_take(src, dst, ss, rs):
        @pl.loop(0, 8)
        def _(n):
            from_dp, from_seq = (n // 2) * 2 + dp // 4, (n % 2) * PLANE + xy

            @pl.when(jnp.logical_not((from_dp == dp) & (from_seq == seq)))
            def _():
                remote(src.at[n], dst.at[n], ss.at[n], rs.at[n], from_dp, from_seq).wait_recv()

    def z_sent(src, dst, ss, rs):
        @pl.loop(0, 8)
        def _(n):
            to_dp, to_seq = z_target(n)

            @pl.when(jnp.logical_not((to_dp == dp) & (to_seq == seq)))
            def _():
                remote(src.at[n], dst.at[n], ss.at[n], rs.at[n], to_dp, to_seq).wait_send()

    z_push(wsend, wrecv, w_ss, w_rs)

    z_take(wsend, wrecv, w_ss, w_rs)
    total = wrecv[0].astype(F32)
    for n in range(1, 8):
        total = total + wrecv[n].astype(F32)
    wsum[0:144, :] = total
    wsum[144:160, :] = jnp.zeros((16, 288), F32)
    for n in range(16):
        begin = (n // 2) * 18
        vsend[n] = wsum[begin : begin + 32, 144 * (n % 2) : 144 * (n % 2) + 144].astype(BF16)

    def v_target(n):
        return z_hi * 2 + n % 2, z_lo * PLANE + 8 * core + n // 2

    @pl.loop(0, 16)
    def _(n):
        to_dp, to_seq = v_target(n)
        own = (to_dp == dp) & (to_seq == seq)

        @pl.when(own)
        def _():
            vrecv[xy] = vsend[n]

        @pl.when(jnp.logical_not(own))
        def _():
            remote(vsend.at[n], vrecv.at[xy], v_ss.at[n], v_rs.at[xy], to_dp, to_seq).start()

    dsum[0:80, :] = dsend[xy].astype(F32)
    dsum[80:96, :] = jnp.zeros((16, 864), F32)

    @pl.loop(1, PLANE)
    def _(k):
        come = (xy + PLANE - k) % PLANE
        remote(
            dsend.at[come], drecv.at[come], d_ss.at[come], d_rs.at[come], dp, z_lo * PLANE + come
        ).wait_recv()
        dsum[0:80, :] += drecv[come].astype(F32)

    for n in range(8):
        begin, column = 36 * (n % 2), 216 * (n // 2)
        zsend[n] = dsum[begin : begin + 48, column : column + 216].astype(BF16)
    z_push(zsend, zrecv, z_ss, z_rs)

    take_all(gbs, gbr, gb_ss, gb_rs)
    unpack(gbr, wide)
    ordered = dot(move, wide[...].astype(BF16), (0, 0))
    gtok[...] = (cot[...].astype(F32) + ordered).astype(BF16)

    @pl.loop(0, 16)
    def _(n):
        from_dp, from_seq = z_hi * 2 + xy // 8, z_lo * PLANE + n

        @pl.when(jnp.logical_not((from_dp == dp) & (from_seq == seq)))
        def _():
            remote(vsend.at[n], vrecv.at[n], v_ss.at[n], v_rs.at[n], from_dp, from_seq).wait_recv()

    total = vrecv[0].astype(F32)
    for n in range(1, 16):
        total = total + vrecv[n].astype(F32)
    gwo[...] = total[:18, :] * FACTOR

    z_take(zsend, zrecv, z_ss, z_rs)
    total = zrecv[0].astype(F32)
    for n in range(1, 8):
        total = total + zrecv[n].astype(F32)
    gwq[...] = total[:36, :] * FACTOR

    sent_all(xs, xr, x_ss, x_rs)
    sent_all(gs, gr, g_ss, g_rs)
    sent_all(ats, atr, at_ss, at_rs)
    sent_all(gbs, gbr, gb_ss, gb_rs)
    swap_cot.wait_send()
    swap_a.wait_send()
    swap_g.wait_send()
    swap_t.wait_send()

    @pl.loop(1, PLANE)
    def _(k):
        plane_copy(k).wait_send()

    z_sent(wsend, wrecv, w_ss, w_rs)
    z_sent(zsend, zrecv, z_ss, z_rs)

    @pl.loop(0, 16)
    def _(n):
        to_dp, to_seq = v_target(n)

        @pl.when(jnp.logical_not((to_dp == dp) & (to_seq == seq)))
        def _():
            remote(vsend.at[n], vrecv.at[n], v_ss.at[n], v_rs.at[n], to_dp, to_seq).wait_send()


def shards(tokens, cotangent, w_qkv, w_out):
    shape = tokens.shape
    vmem = pl.BlockSpec(memory_space=pltpu.VMEM)
    hbm = pl.BlockSpec(memory_space=pl.ANY)
    dma = pltpu.SemaphoreType.DMA
    scratch = [
        ((D, 3 * HD), BF16), ((HD, D), BF16),
        ((ROWS, D), F32), ((ROWS, HD), F32), ((ROWS, D), F32), ((ROWS, D), BF16),
        ((SEQ, 4, D), BF16), ((SEQ, 4, D), BF16), ((SEQ, 4, HD), BF16), ((SEQ, 4, HD), BF16),
        ((SEQ, 4, HD), BF16), ((SEQ, 4, HD), BF16), ((SEQ, 4, D), BF16), ((SEQ, 4, D), BF16),
        ((4, ROWS, 288), BF16), ((2, ROWS, 288), BF16),
        ((D, ROWS), F32), ((80 * PLANE, ROWS), F32),
        ((80 * PLANE, ROWS), BF16), ((80 * PLANE, ROWS), BF16),
        ((2, ROWS, 864), BF16), ((ROWS, 864), BF16), ((HD, ROWS), BF16), ((HD, ROWS), BF16),
        ((HEADS * ROWS, HD), BF16), ((HEADS * ROWS, HD), BF16),
        ((HEADS * ROWS, HD), BF16), ((HEADS * ROWS, HD), BF16),
        ((HEADS * ROWS, ROWS), F32), ((HEADS * ROWS, ROWS), BF16),
        ((PLANE, 80, 864), BF16), ((PLANE, 80, 864), BF16), ((96, 864), F32),
        ((8, 48, 216), BF16), ((8, 48, 216), BF16),
        ((8, 144, 288), BF16), ((8, 144, 288), BF16), ((160, 288), F32),
        ((16, 32, 144), BF16), ((16, 32, 144), BF16),
    ]
    sems = [2] + [SEQ] * 8 + [4, 4, PLANE, PLANE, 8, 8, 8, 8, 16, 16]
    result, gtok, gwq, gwo = pl.pallas_call(
        kernel,
        out_shape=(
            jax.ShapeDtypeStruct((ROWS, D), BF16),
            jax.ShapeDtypeStruct((ROWS, D), BF16),
            jax.ShapeDtypeStruct((36, 216), F32),
            jax.ShapeDtypeStruct((18, 144), F32),
        ),
        in_specs=[vmem, vmem, hbm, hbm],
        out_specs=(vmem,) * 4,
        scratch_shapes=[pltpu.VMEM(s, t) for s, t in scratch] + [dma((n,)) for n in sems],
        compiler_params=pltpu.CompilerParams(
            collective_id=0, has_side_effects=True, vmem_limit_bytes=56 * 1024 * 1024
        ),
    )(tokens.reshape(ROWS, D), cotangent.reshape(ROWS, D), w_qkv, w_out)
    return (result.reshape(shape), gtok.reshape(shape), gwq, gwo)


def solution(mesh):
    in_specs = (P("dp", "seq", None, None), P("dp", "seq", None, None), P(), P())
    out_specs = (
        P("dp", "seq", None, None),
        P("dp", "seq", None, None),
        P("seq", "dp"),
        P("seq", "dp"),
    )
    return jax.shard_map(shards, mesh=mesh, in_specs=in_specs, out_specs=out_specs, check_vma=False)
```

time: 673 us -> 88.8 us (0.13)
  waiting for transfers between devices: 470 us -> 0 us
  blocking collectives: 86.5 us -> 0 us
  Pallas kernels: 0 us -> 74.6 us
  starting transfers between devices: 46.9 us -> 0 us
  matrix products: 20.8 us -> 0 us
  between operations: 16.1 us -> 0.64 us
  local copies, waits for them, and re-layouts: 24.1 us -> 12.6 us
  other arithmetic: 6.86 us -> 0 us
    unnamed x10 -> x0, waiting for transfers between devices: 434 us -> none
    unnamed x1 -> x0, blocking collectives: 86.5 us -> none
    pallas_call x0 -> x1, Pallas kernels: none -> 74.6 us  [shards(): pl.pallas_call(kernel, out_shape=(jax.ShapeDtypeStruct((ROWS, D), BF16),...]
    all_to_all x8 -> x0, starting transfers between devices: 40.3 us -> none  [the longest x1 9.22 us: shards(): lax.all_to_all(grad_attended.reshape(outputs_frames.shape), 'seq', split_...]
    all_to_all x8 -> x0, waiting for transfers between devices: 35.7 us -> none  [the longest x1 6.71 us: shards(): lax.all_to_all(projected[..., inner_width:2 * inner_width], 'seq', split_...]
    dot_general x11 -> x0, matrix products: 19.7 us -> none  [the longest x1 3.32 us: project(): jnp.dot(flat_normed, w_qkv, preferred_element_type=jnp.float32)]
  transfers between devices with their start and end apart: 15 -> 0, of which waited for: 10 -> 0; matrix products, arithmetic and copies ran while one was open for 5% -> 0% of each run, Pallas kernels for 0% -> 0%
where the time goes in v1:
time: 88.8 us; the launch traced here: 87.8 us
  Pallas kernels  74.6 us (84%)
  local copies, waits for them, and re-layouts  12.6 us (14%)
    pallas_call x1, Pallas kernels, shards(): pl.pallas_call(kernel, out_shape=(jax.ShapeDtypeStruct((ROWS, D), BF16),...  74.6 us
    unnamed x5, local copies, waits for them, and re-layouts  12.6 us

profile of v1, /device:TPU:1, one launch (start us, length us, event | category | flops | bytes accessed | tf_op | source)
XLA Modules:
  0.0 87.8 jit_solution(865165924150623184)
XLA Ops:
  0.6 6.4 %copy.8.wqkv_hbm = bf16[1152,1728]{1,0:T(8,128)(2,1)} copy(bf16[1152,1728]{0,1:T(8,128)(2,1)} %param.6) | data formatting | bytes 7962624 | tf_op args[2]
  7.1 74.6 %shard_map.75 = (bf16[128,1152]{1,0:T(8,128)(2,1)}, bf16[128,1152]{1,0:T(8,128)(2,1)}, f32[36,216]{1,0:T(8,128)}, f32[18,144]{1,0:T(8,128)}) custom-call(bf16[128,1152]{1,0:T(8,128)(2,1)} %bitcast.4, bf16[128,1152]{1,0:T(8,128)(2,1)} %bitcast.5, bf16[1152,1728]{1,0:T(8,128)(2,1)} %copy.8.wqkv_hbm, bf16[576,1152]{1,0:T(8,128)(2,1)} %wout_hbm.1), custom_call_target="tpu_custom_call" | custom-call | tf_op jit(solution)/shard_map/pallas_call | solution.py:390
  81.6 1.7 %copy.13 = bf16[1,2,64,1152]{3,2,1,0:T(8,128)(2,1)} copy(bf16[1,2,64,1152]{3,2,1,0:T(8,128)(2,1)} %bitcast.7) | data formatting | bytes 589824
  83.3 1.7 %copy.14 = bf16[1,2,64,1152]{3,2,1,0:T(8,128)(2,1)} copy(bf16[1,2,64,1152]{3,2,1,0:T(8,128)(2,1)} %bitcast.6) | data formatting | bytes 589824
  85.0 1.4 %copy.15 = f32[36,216]{1,0:T(8,128)} copy(f32[36,216]{1,0:T(8,128)} %get-tuple-element.18) | data formatting | bytes 62208
  86.4 1.3 %copy.16 = f32[18,144]{1,0:T(8,128)} copy(f32[18,144]{1,0:T(8,128)} %get-tuple-element.19) | data formatting | bytes 20736

commit v2 on v1

--- a/solution.py
+++ b/solution.py
@@ -34,15 +34,17 @@
     xs, xr, gs, gr, ats, atr, gbs, gbr,
     cotq, cotr, ntr, arr, amine, apart, gph, gpart, tmine, tpart,
     qb, kb, vb, gab, probs, plow,
-    dsend, drecv, dsum, zsend, zrecv, wsend, wrecv, wsum, vsend, vrecv,
+    fsend, frelay, fback, own, hsend, hrecv, zsend, zrecv, wsend, wrecv, wsum, vsend, vrecv,
     wsem, x_ss, x_rs, g_ss, g_rs, at_ss, at_rs, gb_ss, gb_rs, c_ss, c_rs,
-    d_ss, d_rs, z_ss, z_rs, w_ss, w_rs, v_ss, v_rs,
+    f_ss, f_rs, h_ss, h_rs, z_ss, z_rs, w_ss, w_rs, v_ss, v_rs,
 ):
     dp, seq = lax.axis_index("dp"), lax.axis_index("seq")
     core, z_hi = dp % 2, dp // 2
     xy, z_lo = seq % PLANE, seq // PLANE
     mate = z_hi * 2 + 1 - core
     zed = z_hi * 2 + z_lo
+    x, y = xy % 4, xy // 4
+    step = 1 + 2 * core
 
     def remote(src, dst, send_sem, recv_sem, to_dp, to_seq):
         return pltpu.make_async_remote_copy(
@@ -123,16 +125,16 @@
 
     take_all(xs, xr, x_ss, x_rs)
     unpack(xr, wide)
-    x = wide[...]
-    centered = x - jnp.mean(x, axis=-1, keepdims=True)
+    moved = wide[...]
+    centered = moved - jnp.mean(moved, axis=-1, keepdims=True)
     inv_std = lax.rsqrt(jnp.mean(centered * centered, axis=-1, keepdims=True) + EPS)
     x_hat = centered * inv_std
     xhat[...] = x_hat
     load_wqkv.wait()
-    projected = dot(x_hat.astype(BF16), wqkv[...], (1, 0))
-    query = projected[:, :HD].astype(BF16)
-    key = projected[:, HD : 2 * HD].astype(BF16)
-    value = projected[:, 2 * HD :].astype(BF16)
+    normed = x_hat.astype(BF16)
+    query = dot(normed, wqkv[0:HD, :], (1, 1)).astype(BF16)
+    key = dot(normed, wqkv[HD : 2 * HD, :], (1, 1)).astype(BF16)
+    value = dot(normed, wqkv[2 * HD : 3 * HD, :], (1, 1)).astype(BF16)
     lane = lax.broadcasted_iota(jnp.int32, (ROWS, HD), 1)
 
     def stack(block, out):
@@ -160,9 +162,9 @@
 
     ntr[...] = xhat[...].T
     for p in range(PLANE):
-        arr[80 * p : 80 * p + 36, :] = ntr[36 * p : 36 * p + 36, :]
-        arr[80 * p + 36 : 80 * p + 72, :] = ntr[36 * (PLANE + p) : 36 * (PLANE + p) + 36, :]
-        arr[80 * p + 72 : 80 * p + 80, :] = jnp.zeros((8, ROWS), F32)
+        begin = 144 * (p % 4) + 36 * (p // 4)
+        arr[begin : begin + 36, :] = ntr[36 * p : 36 * p + 36, :]
+    arr[576:, :] = ntr[576:, :]
     amine[...] = arr[...].astype(BF16)
     swap_a = remote(amine, apart, c_ss.at[1], c_rs.at[1], mate, seq)
     swap_a.start()
@@ -185,35 +187,6 @@
     swap_g.start()
     grad_proj = grad_proj.astype(BF16)
 
-    swap_a.wait_recv()
-    swap_g.wait_recv()
-    right = jnp.concatenate([gph[core], gpart[...]], axis=0)
-
-    def plane_copy(k):
-        to = (xy + k) % PLANE
-        return remote(
-            dsend.at[to], drecv.at[xy], d_ss.at[to], d_rs.at[xy], dp, z_lo * PLANE + to
-        )
-
-    @pl.loop(1, PLANE + 1)
-    def _(k):
-        to = (xy + k) % PLANE
-        rows = pl.ds(pl.multiple_of(to * 80, 16), 80)
-        left = jnp.concatenate([amine[rows, :], apart[rows, :]], axis=1)
-        dsend[to] = dot(left, right, (1, 0)).astype(BF16)
-
-        @pl.when(k < PLANE)
-        def _():
-            plane_copy(k).start()
-
-    grad_normed = dot(grad_proj, wqkv[...], (1, 1))
-    x_hat = xhat[...]
-    first = jnp.mean(grad_normed, axis=-1, keepdims=True)
-    second = jnp.mean(grad_normed * x_hat, axis=-1, keepdims=True)
-    wide[...] = (grad_normed - first - x_hat * second) * inv_std
-    pack(wide, gbs)
-    push_all(gbs, gbr, gb_ss, gb_rs)
-
     take_all(ats, atr, at_ss, at_rs)
     unpack(atr, slim)
     back = slim[...].astype(BF16)
@@ -223,6 +196,36 @@
     ordered = dot(move, back, (0, 0)).astype(BF16)
     branch = dot(ordered, wout[...], (1, 0))
     result[...] = (tok[...].astype(F32) + branch).astype(BF16)
+    swap_a.wait_recv()
+    swap_g.wait_recv()
+    right_g = jnp.concatenate([gph[core], gpart[...]], axis=0)
+
+    def block(t, to):
+        rows = pl.ds(pl.multiple_of(t * 576 + to * 144, 16), 144)
+        return dot(jnp.concatenate([amine[rows, :], apart[rows, :]], axis=1), right_g, (1, 0))
+
+    def member(t, r):
+        r = r % 4
+        return z_lo * PLANE + (4 * y + r if t == 0 else 4 * r + x)
+
+    ring = (x, y)
+
+    def hop(t, n):
+        src, dst, ahead = (
+            (fsend.at[t, 0, 0:80], frelay.at[t, 0:80], True),
+            (fsend.at[t, 0, 80:144], frelay.at[t, 80:144], False),
+            (fsend.at[t, 1, 0:80], fback.at[t, 0, 0:80], True),
+            (fsend.at[t, 1, 80:144], fback.at[t, 0, 80:144], True),
+            (fsend.at[t, 2, 0:80], fback.at[t, 1, 0:80], False),
+            (fsend.at[t, 2, 80:144], fback.at[t, 1, 80:144], False),
+        )[n]
+        to = ring[t] + (step if ahead else 4 - step)
+        return remote(src, dst, f_ss.at[t, n], f_rs.at[t, n], dp, member(t, to))
+
+    for t in range(2):
+        fsend[t, 0] = block(t, (ring[t] + 2) % 4).astype(BF16)
+        hop(t, 0).start()
+        hop(t, 1).start()
     swap_cot.wait_recv()
     swap_t.wait_recv()
 
@@ -230,9 +233,9 @@
         return 4 * core + n // 2, (n % 2) * PLANE + xy
 
     for j in range(2):
-        right = jnp.concatenate([cotq[2 * core + j], cotr[j]], axis=0)
+        right_c = jnp.concatenate([cotq[2 * core + j], cotr[j]], axis=0)
         left = jnp.concatenate([tmine[...], tpart[...]], axis=1)
-        product = dot(left, right, (1, 0))
+        product = dot(left, right_c, (1, 0))
         for c in range(2):
             for half in range(2):
                 n = (2 * j + c) * 2 + half
@@ -273,6 +276,55 @@
 
     z_push(wsend, wrecv, w_ss, w_rs)
 
+    for t in range(2):
+        fsend[t, 1] = block(t, (ring[t] + step) % 4).astype(BF16)
+        hop(t, 3).start()
+        fsend[t, 2] = block(t, (ring[t] + 4 - step) % 4).astype(BF16)
+        hop(t, 4).start()
+    for t in range(2):
+        own[t, 0:144] = block(t, ring[t])
+        own[t, 144:160] = jnp.zeros((16, 864), F32)
+    for t in range(2):
+        hop(t, 0).wait_recv()
+        fsend[t, 1, 0:80] = (fsend[t, 1, 0:80].astype(F32) + frelay[t, 0:80].astype(F32)).astype(BF16)
+        hop(t, 2).start()
+        hop(t, 1).wait_recv()
+        fsend[t, 2, 80:144] = (
+            fsend[t, 2, 80:144].astype(F32) + frelay[t, 80:144].astype(F32)
+        ).astype(BF16)
+        hop(t, 5).start()
+    grad_normed = dot(grad_proj, wqkv[...], (1, 0))
+    x_hat = xhat[...]
+    first = jnp.mean(grad_normed, axis=-1, keepdims=True)
+    second = jnp.mean(grad_normed * x_hat, axis=-1, keepdims=True)
+    wide[...] = (grad_normed - first - x_hat * second) * inv_std
+    pack(wide, gbs)
+    push_all(gbs, gbr, gb_ss, gb_rs)
+
+    def cross(t, k):
+        to = (ring[1 - t] + k) % 4
+        return remote(
+            hsend.at[t, to], hrecv.at[t, ring[1 - t]], h_ss.at[t, to], h_rs.at[t, ring[1 - t]],
+            dp, member(1 - t, to),
+        )
+
+    for t in range(2):
+        for n in range(2, 6):
+            hop(t, n).wait_recv()
+        own[t, 0:144] += fback[t, 0].astype(F32) + fback[t, 1].astype(F32)
+        for p in range(4):
+            hsend[t, p] = own[t, 36 * p : 36 * p + 48].astype(BF16)
+        for k in (2, 1, 3):
+            cross(t, k).start()
+        hrecv[t, ring[1 - t]] = hsend[t, ring[1 - t]]
+
+    sent_all(xs, xr, x_ss, x_rs)
+    sent_all(gs, gr, g_ss, g_rs)
+    sent_all(ats, atr, at_ss, at_rs)
+    swap_cot.wait_send()
+    swap_a.wait_send()
+    swap_g.wait_send()
+    swap_t.wait_send()
     z_take(wsend, wrecv, w_ss, w_rs)
     total = wrecv[0].astype(F32)
     for n in range(1, 8):
@@ -299,20 +351,18 @@
         def _():
             remote(vsend.at[n], vrecv.at[xy], v_ss.at[n], v_rs.at[xy], to_dp, to_seq).start()
 
-    dsum[0:80, :] = dsend[xy].astype(F32)
-    dsum[80:96, :] = jnp.zeros((16, 864), F32)
-
-    @pl.loop(1, PLANE)
-    def _(k):
-        come = (xy + PLANE - k) % PLANE
-        remote(
-            dsend.at[come], drecv.at[come], d_ss.at[come], d_rs.at[come], dp, z_lo * PLANE + come
-        ).wait_recv()
-        dsum[0:80, :] += drecv[come].astype(F32)
-
-    for n in range(8):
-        begin, column = 36 * (n % 2), 216 * (n // 2)
-        zsend[n] = dsum[begin : begin + 48, column : column + 216].astype(BF16)
+    for t in range(2):
+        for k in range(1, 4):
+            come = (ring[1 - t] + k) % 4
+            remote(
+                hsend.at[t, come], hrecv.at[t, come], h_ss.at[t, come], h_rs.at[t, come],
+                dp, member(1 - t, come),
+            ).wait_recv()
+        total = hrecv[t, 0].astype(F32)
+        for p in range(1, 4):
+            total = total + hrecv[t, p].astype(F32)
+        for j in range(4):
+            zsend[2 * j + t] = total[:, 216 * j : 216 * j + 216].astype(BF16)
     z_push(zsend, zrecv, z_ss, z_rs)
 
     take_all(gbs, gbr, gb_ss, gb_rs)
@@ -339,18 +389,12 @@
         total = total + zrecv[n].astype(F32)
     gwq[...] = total[:36, :] * FACTOR
 
-    sent_all(xs, xr, x_ss, x_rs)
-    sent_all(gs, gr, g_ss, g_rs)
-    sent_all(ats, atr, at_ss, at_rs)
     sent_all(gbs, gbr, gb_ss, gb_rs)
-    swap_cot.wait_send()
-    swap_a.wait_send()
-    swap_g.wait_send()
-    swap_t.wait_send()
-
-    @pl.loop(1, PLANE)
-    def _(k):
-        plane_copy(k).wait_send()
+    for t in range(2):
+        for n in range(6):
+            hop(t, n).wait_send()
+        for k in range(1, 4):
+            cross(t, k).wait_send()
 
     z_sent(wsend, wrecv, w_ss, w_rs)
     z_sent(zsend, zrecv, z_ss, z_rs)
@@ -362,6 +406,11 @@
         @pl.when(jnp.logical_not((to_dp == dp) & (to_seq == seq)))
         def _():
             remote(vsend.at[n], vrecv.at[n], v_ss.at[n], v_rs.at[n], to_dp, to_seq).wait_send()
+
+
+def hand_over(*refs):
+    for n in range(4):
+        refs[4 + n][...] = refs[n][...]
 
 
 def shards(tokens, cotangent, w_qkv, w_out):
@@ -370,38 +419,45 @@
     hbm = pl.BlockSpec(memory_space=pl.ANY)
     dma = pltpu.SemaphoreType.DMA
     scratch = [
-        ((D, 3 * HD), BF16), ((HD, D), BF16),
+        ((3 * HD, D), BF16), ((HD, D), BF16),
         ((ROWS, D), F32), ((ROWS, HD), F32), ((ROWS, D), F32), ((ROWS, D), BF16),
         ((SEQ, 4, D), BF16), ((SEQ, 4, D), BF16), ((SEQ, 4, HD), BF16), ((SEQ, 4, HD), BF16),
         ((SEQ, 4, HD), BF16), ((SEQ, 4, HD), BF16), ((SEQ, 4, D), BF16), ((SEQ, 4, D), BF16),
         ((4, ROWS, 288), BF16), ((2, ROWS, 288), BF16),
-        ((D, ROWS), F32), ((80 * PLANE, ROWS), F32),
-        ((80 * PLANE, ROWS), BF16), ((80 * PLANE, ROWS), BF16),
+        ((D, ROWS), F32), ((D, ROWS), F32), ((D, ROWS), BF16), ((D, ROWS), BF16),
         ((2, ROWS, 864), BF16), ((ROWS, 864), BF16), ((HD, ROWS), BF16), ((HD, ROWS), BF16),
         ((HEADS * ROWS, HD), BF16), ((HEADS * ROWS, HD), BF16),
         ((HEADS * ROWS, HD), BF16), ((HEADS * ROWS, HD), BF16),
         ((HEADS * ROWS, ROWS), F32), ((HEADS * ROWS, ROWS), BF16),
-        ((PLANE, 80, 864), BF16), ((PLANE, 80, 864), BF16), ((96, 864), F32),
+        ((2, 3, 144, 864), BF16), ((2, 144, 864), BF16), ((2, 2, 144, 864), BF16), ((2, 160, 864), F32),
+        ((2, 4, 48, 864), BF16), ((2, 4, 48, 864), BF16),
         ((8, 48, 216), BF16), ((8, 48, 216), BF16),
         ((8, 144, 288), BF16), ((8, 144, 288), BF16), ((160, 288), F32),
         ((16, 32, 144), BF16), ((16, 32, 144), BF16),
     ]
-    sems = [2] + [SEQ] * 8 + [4, 4, PLANE, PLANE, 8, 8, 8, 8, 16, 16]
-    result, gtok, gwq, gwo = pl.pallas_call(
+    sems = [(2,)] + [(SEQ,)] * 8 + [(4,)] * 2 + [(2, 6)] * 2 + [(2, 4)] * 2 + [(8,)] * 4 + [(16,)] * 2
+    out_shape = (
+        jax.ShapeDtypeStruct((ROWS, D), BF16),
+        jax.ShapeDtypeStruct((ROWS, D), BF16),
+        jax.ShapeDtypeStruct((36, 216), F32),
+        jax.ShapeDtypeStruct((18, 144), F32),
+    )
+    outs = pl.pallas_call(
         kernel,
-        out_shape=(
-            jax.ShapeDtypeStruct((ROWS, D), BF16),
-            jax.ShapeDtypeStruct((ROWS, D), BF16),
-            jax.ShapeDtypeStruct((36, 216), F32),
-            jax.ShapeDtypeStruct((18, 144), F32),
-        ),
+        out_shape=out_shape,
         in_specs=[vmem, vmem, hbm, hbm],
         out_specs=(vmem,) * 4,
-        scratch_shapes=[pltpu.VMEM(s, t) for s, t in scratch] + [dma((n,)) for n in sems],
+        scratch_shapes=[pltpu.VMEM(s, t) for s, t in scratch] + [dma(n) for n in sems],
         compiler_params=pltpu.CompilerParams(
             collective_id=0, has_side_effects=True, vmem_limit_bytes=56 * 1024 * 1024
         ),
-    )(tokens.reshape(ROWS, D), cotangent.reshape(ROWS, D), w_qkv, w_out)
+    )(tokens.reshape(ROWS, D), cotangent.reshape(ROWS, D), w_qkv.T, w_out)
+    result, gtok, gwq, gwo = pl.pallas_call(
+        hand_over,
+        out_shape=out_shape,
+        in_specs=[vmem] * 4,
+        out_specs=(vmem,) * 4,
+    )(*outs)
     return (result.reshape(shape), gtok.reshape(shape), gwq, gwo)
 
 

time: 88.8 us -> 67.7 us (0.76)
  local copies, waits for them, and re-layouts: 12.6 us -> 0 us
  Pallas kernels: 74.6 us -> 66.9 us
    unnamed x5 -> x0, local copies, waits for them, and re-layouts: 12.6 us -> none
    pallas_call x1 -> x2, Pallas kernels: 74.6 us -> 66.9 us  [the longest x1 65 us: shards(): pl.pallas_call(kernel, out_shape=out_shape, in_specs=[vmem, vmem, hbm, hb...]
where the time goes in v2:
time: 67.7 us; the launch traced here: 67.6 us
  Pallas kernels  66.9 us (99%)
    pallas_call x1, Pallas kernels, shards(): pl.pallas_call(kernel, out_shape=out_shape, in_specs=[vmem, vmem, hbm, hb...  65 us
    pallas_call x1, Pallas kernels, shards(): pl.pallas_call(hand_over, out_shape=out_shape, in_specs=[vmem] * 4, out_s...  1.9 us

profile of v2, /device:TPU:1, one launch (start us, length us, event | category | flops | bytes accessed | tf_op | source)
XLA Modules:
  0.0 67.6 jit_solution(6424209783897991378)
XLA Ops:
  0.6 65.0 %shard_map.75 = (bf16[128,1152]{1,0:T(8,128)(2,1)}, bf16[128,1152]{1,0:T(8,128)(2,1)}, f32[36,216]{1,0:T(8,128)}, f32[18,144]{1,0:T(8,128)}) custom-call(bf16[128,1152]{1,0:T(8,128)(2,1)} %bitcast.6, bf16[128,1152]{1,0:T(8,128)(2,1)} %bitcast.7, bf16[1728,1152]{1,0:T(8,128)(2,1)} %bitcast.5, bf16[576,1152]{1,0:T(8,128)(2,1)} %wout_hbm.1), custom_call_target="tpu_custom_call" | custom-call | tf_op jit(solution)/shard_map/pallas_call | solution.py:445
  65.7 1.9 %shard_map.76 = (bf16[128,1152]{1,0:T(8,128)(2,1)}, bf16[128,1152]{1,0:T(8,128)(2,1)}, f32[36,216]{1,0:T(8,128)}, f32[18,144]{1,0:T(8,128)}) custom-call(bf16[128,1152]{1,0:T(8,128)(2,1)} %get-tuple-element.12.refs_0_, bf16[128,1152]{1,0:T(8,128)(2,1)} %get-tuple-element.13.refs_1_, f32[36,216]{1,0:T(8,128)} %get-tuple-element.14.refs_2_, ...), custom_call_target="tpu_custom_call" | custom-call | tf_op jit(solution)/shard_map/pallas_call | solution.py:455

commit v3 on v2

v3 whole, which is shorter than its diff:
```python
import functools

import jax
import jax.numpy as jnp
from jax import lax
from jax.experimental import pallas as pl
from jax.experimental.pallas import tpu as pltpu
from jax.sharding import PartitionSpec as P

MESH = pl.DeviceIdType.MESH
F32, BF16 = jnp.float32, jnp.bfloat16

D = 1152
HEADS = 8
HS = 72
HD = 576
ROWS = 128
SEQ = 32
PLANE = 16
EPS = 1e-6
SCALE = HS ** (-0.5)
FACTOR = 32768 ** (-0.5)


def dot(a, b, contract):
    return lax.dot_general(a, b, ((contract[:1], contract[1:]), ((), ())), preferred_element_type=F32)


def kernel(
    tok_hbm, cot_hbm, wqkv_hbm, wout_hbm,
    result_hbm, gtok_hbm, gwq, gwo,
    tok, cot, wqkv, wout, result, gtok,
    wide, slim, xhat, cotp,
    xs, xr, gs, gr, ats, atr, gbs, gbr,
    cots, cotr, ntr, arr, amine, apart, gph, gpart, ttr, tarr, tmine, tpart,
    qb, kb, vb, gab, probs, plow,
    fsend0, frelay0, fback0, own0, fsend1, frelay1, fback1, own1, hsend, hrecv, zsend, zrecv,
    wsem, a_ss, a_rs, c_ss, c_rs, f_ss, f_rs, h_ss, h_rs, z_ss, z_rs,
):
    dp, seq = lax.axis_index("dp"), lax.axis_index("seq")
    core, z_hi = dp % 2, dp // 2
    xy, z_lo = seq % PLANE, seq // PLANE
    mate = z_hi * 2 + 1 - core
    zed = z_hi * 2 + z_lo
    x, y = xy % 4, xy // 4
    step = 1 + 2 * core

    def remote(src, dst, send_sem, recv_sem, to_dp, to_seq):
        return pltpu.make_async_remote_copy(
            src_ref=src, dst_ref=dst, send_sem=send_sem, recv_sem=recv_sem,
            device_id=(to_dp, to_seq), device_id_type=MESH,
        )

    barrier = pltpu.get_barrier_semaphore()

    def greet(to_dp, to_seq):
        pl.semaphore_signal(barrier, inc=1, device_id=(to_dp, to_seq), device_id_type=MESH)

    @pl.loop(1, SEQ)
    def _(k):
        greet(dp, (seq + k) % SEQ)

    @pl.loop(1, 8)
    def _(k):
        greet((dp + k) % 8, xy)
        greet((dp + k) % 8, PLANE + xy)

    load_wqkv = pltpu.make_async_copy(wqkv_hbm, wqkv, wsem.at[0])
    load_wout = pltpu.make_async_copy(wout_hbm, wout, wsem.at[1])
    load_tok = pltpu.make_async_copy(tok_hbm, tok, wsem.at[2])
    load_cot = pltpu.make_async_copy(cot_hbm, cot, wsem.at[3])
    load_tok.start()
    load_cot.start()
    load_wout.start()
    load_wqkv.start()

    new = lax.broadcasted_iota(jnp.int32, (ROWS, ROWS), 0)
    old = lax.broadcasted_iota(jnp.int32, (ROWS, ROWS), 1)
    place = ((new >> 1) & 1) * 64 + (new >> 2) * 2 + (new & 1)
    move = jnp.where(place == old, 1.0, 0.0).astype(BF16)

    def pack(rows, block):
        for p in range(SEQ):
            block[p] = rows[4 * p : 4 * p + 4, :].astype(BF16)

    def unpack(block, rows):
        for p in range(SEQ):
            rows[4 * p : 4 * p + 4, :] = block[p].astype(F32)

    def push_all(src, dst, e):
        @pl.loop(1, SEQ)
        def _(k):
            to = (seq + k) % SEQ
            remote(src.at[to], dst.at[seq], a_ss.at[e], a_rs.at[e], dp, to).start()

        pltpu.make_async_copy(src.at[seq], dst.at[seq], a_rs.at[e]).start()

    def take_all(src, dst, e):
        pltpu.make_async_copy(src, dst, a_rs.at[e]).wait()

    def sent_all(src, dst, e):
        many = pl.ds(0, SEQ - 1)
        remote(src.at[many], dst.at[many], a_ss.at[e], a_rs.at[e], dp, (seq + 1) % SEQ).wait_send()

    load_tok.wait()
    wide[...] = dot(move, tok[...], (1, 0))
    pack(wide, xs)
    pl.semaphore_wait(barrier, SEQ - 1 + 14)
    push_all(xs, xr, 0)

    load_cot.wait()
    cotp[...] = dot(move, cot[...], (1, 0)).astype(BF16)
    load_wout.wait()
    slim[...] = dot(cotp[...], wout[...], (1, 1))
    pack(slim, gs)
    push_all(gs, gr, 1)
    for c in range(2):
        half = cotp[:, HD * c : HD * c + HD].astype(F32)
        gap0, gap1 = jnp.zeros((ROWS, 72), F32), jnp.zeros((ROWS, 144), F32)
        whole, left, right = [], [], []
        for j in range(4):
            b = 144 * j
            whole += [half[:, b : b + 144], gap0]
            left += [gap1, half[:, b : b + 72]]
            right += [gap1, half[:, b + 72 : b + 144]]
        for n, parts in enumerate((whole, left, right)):
            cots[c, n * ROWS : (n + 1) * ROWS, :] = jnp.concatenate(parts, axis=1).astype(BF16)
    swap_cot = remote(cots.at[1 - core], cotr, c_ss.at[0], c_rs.at[0], mate, seq)
    swap_cot.start()

    take_all(xs, xr, 0)
    unpack(xr, wide)
    moved = wide[...]
    centered = moved - jnp.mean(moved, axis=-1, keepdims=True)
    inv_std = lax.rsqrt(jnp.mean(centered * centered, axis=-1, keepdims=True) + EPS)
    x_hat = centered * inv_std
    xhat[...] = x_hat
    load_wqkv.wait()
    normed = x_hat.astype(BF16)
    query = dot(normed, wqkv[0:HD, :], (1, 1)).astype(BF16)
    key = dot(normed, wqkv[HD : 2 * HD, :], (1, 1)).astype(BF16)
    value = dot(normed, wqkv[2 * HD : 3 * HD, :], (1, 1)).astype(BF16)
    lane = lax.broadcasted_iota(jnp.int32, (ROWS, HD), 1)

    def stack(block, out):
        wide_block = block.astype(F32)
        for h in range(HEADS):
            inside = (lane >= h * HS) & (lane < (h + 1) * HS)
            out[h * ROWS : (h + 1) * ROWS, :] = jnp.where(inside, wide_block, 0.0).astype(BF16)

    def side(block):
        return jnp.concatenate([block[h * ROWS : (h + 1) * ROWS, :] for h in range(HEADS)], axis=1)

    stack(query, qb)
    stack(value, vb)
    scores = dot(qb[...], key, (1, 1)) * SCALE
    here = lax.broadcasted_iota(jnp.int32, (HEADS * ROWS, ROWS), 0)
    there = lax.broadcasted_iota(jnp.int32, (HEADS * ROWS, ROWS), 1)
    scores = jnp.where(((here ^ there) & 1) == 0, scores, -jnp.inf)
    expo = jnp.exp(scores - jnp.max(scores, axis=-1, keepdims=True))
    prob = expo / jnp.sum(expo, axis=-1, keepdims=True)
    probs[...] = prob
    plow[...] = prob.astype(BF16)
    slim[...] = dot(side(plow), vb[...], (1, 0))
    pack(slim, ats)
    push_all(ats, atr, 2)

    ntr[...] = xhat[...].T
    for p in range(PLANE):
        begin = 144 * (p % 4) + 36 * (p // 4)
        arr[begin : begin + 36, :] = ntr[36 * p : 36 * p + 36, :]
    arr[576:, :] = ntr[576:, :]
    amine[...] = arr[...].astype(BF16)
    swap_a = remote(amine, apart, c_ss.at[1], c_rs.at[1], mate, seq)
    swap_a.start()

    stack(key, kb)
    take_all(gs, gr, 1)
    unpack(gr, slim)
    stack(slim[...], gab)
    grad_probs = dot(gab[...], value, (1, 1))
    prob = probs[...]
    delta = jnp.sum(prob * grad_probs, axis=-1, keepdims=True)
    grad_scores = (prob * (grad_probs - delta) * SCALE).astype(BF16)
    grad_query = dot(side(grad_scores), kb[...], (1, 0))
    grad_key = dot(grad_scores, qb[...], (0, 0))
    grad_value = dot(plow[...], gab[...], (0, 0))
    grad_proj = jnp.concatenate([grad_query, grad_key, grad_value], axis=1)
    gph[0] = grad_proj[:, :864].astype(BF16)
    gph[1] = grad_proj[:, 864:].astype(BF16)
    swap_g = remote(gph.at[1 - core], gpart, c_ss.at[2], c_rs.at[2], mate, seq)
    swap_g.start()
    grad_proj = grad_proj.astype(BF16)

    grad_normed = dot(grad_proj, wqkv[...], (1, 0))
    x_hat = xhat[...]
    first = jnp.mean(grad_normed, axis=-1, keepdims=True)
    second = jnp.mean(grad_normed * x_hat, axis=-1, keepdims=True)
    wide[...] = (grad_normed - first - x_hat * second) * inv_std
    pack(wide, gbs)
    swap_a.wait_recv()
    swap_g.wait_recv()

    size, part, piece = (144, 48), (80, 32), (36, 12)
    fsend, frelay, fback, own = (fsend0, fsend1), (frelay0, frelay1), (fback0, fback1), (own0, own1)
    ring = (x, y)

    def member(t, r):
        r = r % 4
        return z_lo * PLANE + (4 * y + r if t == 0 else 4 * r + x)

    def block(kind, t, to):
        mine, theirs = ((amine, apart), (tmine, tpart))[kind]
        n = size[kind]
        rows = pl.ds(pl.multiple_of((t * 4 + to) * n, 16), n)
        if kind == 0:
            right = jnp.concatenate([gph[core], gpart[...]], axis=0)
        else:
            right = jnp.concatenate([cots[core], cotr[...]], axis=0)
        return dot(jnp.concatenate([mine[rows, :], theirs[rows, :]], axis=1), right, (1, 0))

    def hop(kind, t, n):
        send, relay, back = fsend[kind], frelay[kind], fback[kind]
        half = (slice(0, part[kind]), slice(part[kind], size[kind]))[n % 2]
        dst = relay.at[t, half] if n < 2 else back.at[t, n // 2 - 1, half]
        ahead = n in (0, 2, 3)
        to = ring[t] + (step if ahead else 4 - step)
        return remote(
            send.at[t, n // 2, half], dst, f_ss.at[kind, t, n], f_rs.at[kind, t, n], dp, member(t, to)
        )

    def opposite(kind):
        for t in range(2):
            fsend[kind][t, 0] = block(kind, t, (ring[t] + 2) % 4).astype(BF16)
            hop(kind, t, 0).start()
            hop(kind, t, 1).start()

    def near(kind):
        for t in range(2):
            fsend[kind][t, 1] = block(kind, t, (ring[t] + step) % 4).astype(BF16)
            hop(kind, t, 3).start()
            fsend[kind][t, 2] = block(kind, t, (ring[t] + 4 - step) % 4).astype(BF16)
            hop(kind, t, 4).start()

    def stay(kind):
        for t in range(2):
            own[kind][t] = block(kind, t, ring[t])

    def relays(kind):
        send, relay, cut = fsend[kind], frelay[kind], part[kind]
        for t in range(2):
            for n, half in ((0, slice(0, cut)), (1, slice(cut, size[kind]))):
                hop(kind, t, n).wait_recv()
                send[t, 1 + n, half] = (
                    send[t, 1 + n, half].astype(F32) + relay[t, half].astype(F32)
                ).astype(BF16)
                hop(kind, t, 2 + 3 * n).start()

    def arrived(kind):
        for t in range(2):
            for n in range(2, 6):
                hop(kind, t, n).wait_recv()
            own[kind][t] += fback[kind][t, 0].astype(F32) + fback[kind][t, 1].astype(F32)

    def cross():
        for t in range(2):
            here = ring[1 - t]
            for p in range(4):
                hsend[t, p] = jnp.concatenate(
                    [own0[t, 36 * p : 36 * p + 36], own1[t, 12 * p : 12 * p + 12]], axis=0
                ).astype(BF16)
            for k in (2, 1, 3):
                to = (here + k) % 4
                remote(
                    hsend.at[t, to], hrecv.at[t, here], h_ss.at[t], h_rs.at[t], dp, member(1 - t, to)
                ).start()
            pltpu.make_async_copy(hsend.at[t, here], hrecv.at[t, here], h_rs.at[t]).start()

    def z_target(n):
        return 4 * core + n // 2, (n % 2) * PLANE + xy

    def crossed():
        for t in range(2):
            pltpu.make_async_copy(hsend.at[t], hrecv.at[t], h_rs.at[t]).wait()
            total = hrecv[t, 0].astype(F32)
            for p in range(1, 4):
                total = total + hrecv[t, p].astype(F32)
            for j in range(4):
                zsend[2 * j + t] = total[:, 216 * j : 216 * j + 216].astype(BF16)

        @pl.loop(0, 8)
        def _(n):
            to_dp, to_seq = z_target(n)
            is_me = (to_dp == dp) & (to_seq == seq)

            @pl.when(is_me)
            def _():
                pltpu.make_async_copy(zsend.at[n], zrecv.at[zed], z_rs.at[0]).start()

            @pl.when(jnp.logical_not(is_me))
            def _():
                remote(zsend.at[n], zrecv.at[zed], z_ss.at[0], z_rs.at[0], to_dp, to_seq).start()

    def gathered():
        pltpu.make_async_copy(zsend, zrecv, z_rs.at[0]).wait()
        total = zrecv[0].astype(F32)
        for n in range(1, 8):
            total = total + zrecv[n].astype(F32)
        return total * FACTOR

    def z_sent(count):
        many = pl.ds(0, count)
        remote(
            zsend.at[many], zrecv.at[many], z_ss.at[0], z_rs.at[0], mate, seq
        ).wait_send()

    def all_sent():
        for t in range(2):
            for kind in range(2):
                for n in range(6):
                    hop(kind, t, n).wait_send()
            many = pl.ds(0, 3)
            remote(
                hsend.at[t, many], hrecv.at[t, many], h_ss.at[t], h_rs.at[t], dp, member(1 - t, ring[1 - t] + 1)
            ).wait_send()
        pl.when(z_hi // 2 == core)(lambda: z_sent(7))
        pl.when(z_hi // 2 != core)(lambda: z_sent(8))

    opposite(0)
    near(0)
    take_all(ats, atr, 2)
    unpack(atr, slim)
    ttr[...] = slim[...].T
    tarr[...] = jnp.zeros((384, 3 * ROWS), F32)
    for p in range(2 * PLANE):
        if p < PLANE:
            begin = 48 * (p % 4) + 12 * (p // 4)
        else:
            begin = 12 * p
        tarr[begin : begin + 12, 0:ROWS] = ttr[18 * p : 18 * p + 12, :]
        rest = ttr[18 * p + 12 : 18 * p + 18, :]
        tarr[begin : begin + 6, ROWS : 2 * ROWS] = rest
        tarr[begin + 6 : begin + 12, 2 * ROWS :] = rest
    tmine[...] = tarr[...].astype(BF16)
    swap_t = remote(tmine, tpart, c_ss.at[3], c_rs.at[3], mate, seq)
    swap_t.start()
    stay(0)
    swap_cot.wait_recv()
    swap_t.wait_recv()
    opposite(1)
    relays(0)
    near(1)
    ordered = dot(move, slim[...].astype(BF16), (0, 0)).astype(BF16)
    branch = dot(ordered, wout[...], (1, 0))
    result[...] = (tok[...].astype(F32) + branch).astype(BF16)
    store_result = pltpu.make_async_copy(result, result_hbm, wsem.at[4])
    store_result.start()
    relays(1)
    stay(1)
    sent_all(xs, xr, 0)
    sent_all(gs, gr, 1)
    sent_all(ats, atr, 2)
    swap_cot.wait_send()
    swap_a.wait_send()
    swap_g.wait_send()
    swap_t.wait_send()
    arrived(0)
    arrived(1)
    cross()
    push_all(gbs, gbr, 3)
    crossed()
    take_all(gbs, gbr, 3)
    unpack(gbr, wide)
    ordered = dot(move, wide[...].astype(BF16), (0, 0))
    gtok[...] = (cot[...].astype(F32) + ordered).astype(BF16)
    store_gtok = pltpu.make_async_copy(gtok, gtok_hbm, wsem.at[5])
    store_gtok.start()
    sent_all(gbs, gbr, 3)
    owned = gathered()
    gwq[...] = owned[:36, :]
    gwo[0:12, :] = owned[36:48, 0:144]
    gwo[12:18, :] = jnp.concatenate([owned[36:42, 144:216], owned[42:48, 144:216]], axis=1)
    all_sent()
    store_result.wait()
    store_gtok.wait()


def hand_over(*refs):
    for n in range(4):
        refs[4 + n][...] = refs[n][...]


def shards(tokens, cotangent, w_qkv, w_out):
    shape = tokens.shape
    vmem = pl.BlockSpec(memory_space=pltpu.VMEM)
    hbm = pl.BlockSpec(memory_space=pl.ANY)
    dma = pltpu.SemaphoreType.DMA
    scratch = [
        ((ROWS, D), BF16), ((ROWS, D), BF16), ((3 * HD, D), BF16), ((HD, D), BF16),
        ((ROWS, D), BF16), ((ROWS, D), BF16),
        ((ROWS, D), F32), ((ROWS, HD), F32), ((ROWS, D), F32), ((ROWS, D), BF16),
        ((SEQ, 4, D), BF16), ((SEQ, 4, D), BF16), ((SEQ, 4, HD), BF16), ((SEQ, 4, HD), BF16),
        ((SEQ, 4, HD), BF16), ((SEQ, 4, HD), BF16), ((SEQ, 4, D), BF16), ((SEQ, 4, D), BF16),
        ((2, 3 * ROWS, 864), BF16), ((3 * ROWS, 864), BF16),
        ((D, ROWS), F32), ((D, ROWS), F32), ((D, ROWS), BF16), ((D, ROWS), BF16),
        ((2, ROWS, 864), BF16), ((ROWS, 864), BF16), ((HD, ROWS), F32), ((384, 3 * ROWS), F32), ((384, 3 * ROWS), BF16), ((384, 3 * ROWS), BF16),
        ((HEADS * ROWS, HD), BF16), ((HEADS * ROWS, HD), BF16),
        ((HEADS * ROWS, HD), BF16), ((HEADS * ROWS, HD), BF16),
        ((HEADS * ROWS, ROWS), F32), ((HEADS * ROWS, ROWS), BF16),
        ((2, 3, 144, 864), BF16), ((2, 144, 864), BF16), ((2, 2, 144, 864), BF16), ((2, 144, 864), F32),
        ((2, 3, 48, 864), BF16), ((2, 48, 864), BF16), ((2, 2, 48, 864), BF16), ((2, 48, 864), F32),
        ((2, 4, 48, 864), BF16), ((2, 4, 48, 864), BF16), ((8, 48, 216), BF16), ((8, 48, 216), BF16),
    ]
    sems = [(6,), (4,), (4,), (4,), (4,), (2, 2, 6), (2, 2, 6), (2,), (2,), (1,), (1,)]
    out_shape = (
        jax.ShapeDtypeStruct((ROWS, D), BF16),
        jax.ShapeDtypeStruct((ROWS, D), BF16),
        jax.ShapeDtypeStruct((36, 216), F32),
        jax.ShapeDtypeStruct((18, 144), F32),
    )
    outs = pl.pallas_call(
        kernel,
        out_shape=out_shape,
        in_specs=[hbm] * 4,
        out_specs=(hbm, hbm, vmem, vmem),
        scratch_shapes=[pltpu.VMEM(s, t) for s, t in scratch] + [dma(n) for n in sems],
        compiler_params=pltpu.CompilerParams(
            collective_id=0, has_side_effects=True, vmem_limit_bytes=56 * 1024 * 1024
        ),
    )(tokens.reshape(ROWS, D), cotangent.reshape(ROWS, D), w_qkv.T, w_out)
    result, gtok, gwq, gwo = pl.pallas_call(
        hand_over,
        out_shape=out_shape,
        in_specs=[vmem] * 4,
        out_specs=(vmem,) * 4,
    )(*outs)
    return (result.reshape(shape), gtok.reshape(shape), gwq, gwo)


def solution(mesh):
    in_specs = (P("dp", "seq", None, None), P("dp", "seq", None, None), P(), P())
    out_specs = (
        P("dp", "seq", None, None),
        P("dp", "seq", None, None),
        P("seq", "dp"),
        P("seq", "dp"),
    )
    return jax.shard_map(shards, mesh=mesh, in_specs=in_specs, out_specs=out_specs, check_vma=False)
```

time: 67.7 us -> 58.8 us (0.87)
  Pallas kernels: 66.9 us -> 58.1 us
    pallas_call x1, Pallas kernels: 65 us -> 56.2 us  [shards(): pl.pallas_call(kernel, out_shape=out_shape, in_specs=[hbm] * 4, out_specs...]
where the time goes in v3:
time: 58.8 us; the launch traced here: 58.7 us
  Pallas kernels  58.1 us (99%)
  between operations  0.64 us (1%)
    pallas_call x1, Pallas kernels, shards(): pl.pallas_call(kernel, out_shape=out_shape, in_specs=[hbm] * 4, out_specs...  56.2 us
    pallas_call x1, Pallas kernels, shards(): pl.pallas_call(hand_over, out_shape=out_shape, in_specs=[vmem] * 4, out_s...  1.9 us

profile of v3, /device:TPU:1, one launch (start us, length us, event | category | flops | bytes accessed | tf_op | source)
XLA Modules:
  0.0 58.7 jit_solution(11103759037401081922)
XLA Ops:
  0.6 56.2 %shard_map.75 = (bf16[128,1152]{1,0:T(8,128)(2,1)}, bf16[128,1152]{1,0:T(8,128)(2,1)}, f32[36,216]{1,0:T(8,128)}, f32[18,144]{1,0:T(8,128)}) custom-call(bf16[128,1152]{1,0:T(8,128)(2,1)} %bitcast.6, bf16[128,1152]{1,0:T(8,128)(2,1)} %bitcast.7, bf16[1728,1152]{1,0:T(8,128)(2,1)} %bitcast.5, bf16[576,1152]{1,0:T(8,128)(2,1)} %wout_hbm.1), custom_call_target="tpu_custom_call" | custom-call | tf_op jit(solution)/shard_map/pallas_call | solution.py:421
  56.8 1.9 %shard_map.76 = (bf16[128,1152]{1,0:T(8,128)(2,1)}, bf16[128,1152]{1,0:T(8,128)(2,1)}, f32[36,216]{1,0:T(8,128)}, f32[18,144]{1,0:T(8,128)}) custom-call(bf16[128,1152]{1,0:T(8,128)(2,1)} %get-tuple-element.12.refs_0_, bf16[128,1152]{1,0:T(8,128)(2,1)} %get-tuple-element.13.refs_1_, f32[36,216]{1,0:T(8,128)} %get-tuple-element.14.refs_2_, ...), custom_call_target="tpu_custom_call" | custom-call | tf_op jit(solution)/shard_map/pallas_call | solution.py:431

commit v4 on v3

--- a/solution.py
+++ b/solution.py
@@ -198,6 +198,14 @@
     second = jnp.mean(grad_normed * x_hat, axis=-1, keepdims=True)
     wide[...] = (grad_normed - first - x_hat * second) * inv_std
     pack(wide, gbs)
+
+    def push_rows(to):
+        remote(gbs.at[to], gbr.at[seq], a_ss.at[3], a_rs.at[3], dp, to).start()
+
+    @pl.loop(0, PLANE)
+    def _(k):
+        push_rows((1 - z_lo) * PLANE + (xy + k) % PLANE)
+
     swap_a.wait_recv()
     swap_g.wait_recv()
 
@@ -226,7 +234,7 @@
         ahead = n in (0, 2, 3)
         to = ring[t] + (step if ahead else 4 - step)
         return remote(
-            send.at[t, n // 2, half], dst, f_ss.at[kind, t, n], f_rs.at[kind, t, n], dp, member(t, to)
+            send.at[t, n // 2, half], dst, f_ss.at[kind], f_rs.at[kind, t, min(n // 2, 1)], dp, member(t, to)
         )
 
     def opposite(kind):
@@ -238,8 +246,11 @@
     def near(kind):
         for t in range(2):
             fsend[kind][t, 1] = block(kind, t, (ring[t] + step) % 4).astype(BF16)
+            fsend[kind][t, 2] = block(kind, t, (ring[t] + 4 - step) % 4).astype(BF16)
+
+    def near_push(kind):
+        for t in range(2):
             hop(kind, t, 3).start()
-            fsend[kind][t, 2] = block(kind, t, (ring[t] + 4 - step) % 4).astype(BF16)
             hop(kind, t, 4).start()
 
     def stay(kind):
@@ -249,8 +260,8 @@
     def relays(kind):
         send, relay, cut = fsend[kind], frelay[kind], part[kind]
         for t in range(2):
+            pltpu.make_async_copy(relay.at[t], relay.at[t], f_rs.at[kind, t, 0]).wait()
             for n, half in ((0, slice(0, cut)), (1, slice(cut, size[kind]))):
-                hop(kind, t, n).wait_recv()
                 send[t, 1 + n, half] = (
                     send[t, 1 + n, half].astype(F32) + relay[t, half].astype(F32)
                 ).astype(BF16)
@@ -258,8 +269,8 @@
 
     def arrived(kind):
         for t in range(2):
-            for n in range(2, 6):
-                hop(kind, t, n).wait_recv()
+            back = fback[kind].at[t]
+            pltpu.make_async_copy(back, back, f_rs.at[kind, t, 1]).wait()
             own[kind][t] += fback[kind][t, 0].astype(F32) + fback[kind][t, 1].astype(F32)
 
     def cross():
@@ -315,10 +326,10 @@
         ).wait_send()
 
     def all_sent():
-        for t in range(2):
-            for kind in range(2):
-                for n in range(6):
-                    hop(kind, t, n).wait_send()
+        for kind in range(2):
+            whole = fsend[kind]
+            remote(whole, whole, f_ss.at[kind], f_rs.at[kind, 0, 0], mate, seq).wait_send()
+        for t in range(2):
             many = pl.ds(0, 3)
             remote(
                 hsend.at[t, many], hrecv.at[t, many], h_ss.at[t], h_rs.at[t], dp, member(1 - t, ring[1 - t] + 1)
@@ -327,7 +338,6 @@
         pl.when(z_hi // 2 != core)(lambda: z_sent(8))
 
     opposite(0)
-    near(0)
     take_all(ats, atr, 2)
     unpack(atr, slim)
     ttr[...] = slim[...].T
@@ -344,19 +354,22 @@
     tmine[...] = tarr[...].astype(BF16)
     swap_t = remote(tmine, tpart, c_ss.at[3], c_rs.at[3], mate, seq)
     swap_t.start()
-    stay(0)
+    near(0)
+    near_push(0)
     swap_cot.wait_recv()
     swap_t.wait_recv()
     opposite(1)
+    near(1)
     relays(0)
-    near(1)
+    near_push(1)
+    stay(0)
+    relays(1)
+    stay(1)
     ordered = dot(move, slim[...].astype(BF16), (0, 0)).astype(BF16)
     branch = dot(ordered, wout[...], (1, 0))
     result[...] = (tok[...].astype(F32) + branch).astype(BF16)
     store_result = pltpu.make_async_copy(result, result_hbm, wsem.at[4])
     store_result.start()
-    relays(1)
-    stay(1)
     sent_all(xs, xr, 0)
     sent_all(gs, gr, 1)
     sent_all(ats, atr, 2)
@@ -367,8 +380,12 @@
     arrived(0)
     arrived(1)
     cross()
-    push_all(gbs, gbr, 3)
     crossed()
+    @pl.loop(1, PLANE)
+    def _(k):
+        push_rows(z_lo * PLANE + (xy + k) % PLANE)
+
+    pltpu.make_async_copy(gbs.at[seq], gbr.at[seq], a_rs.at[3]).start()
     take_all(gbs, gbr, 3)
     unpack(gbr, wide)
     ordered = dot(move, wide[...].astype(BF16), (0, 0))
@@ -411,7 +428,7 @@
         ((2, 3, 48, 864), BF16), ((2, 48, 864), BF16), ((2, 2, 48, 864), BF16), ((2, 48, 864), F32),
         ((2, 4, 48, 864), BF16), ((2, 4, 48, 864), BF16), ((8, 48, 216), BF16), ((8, 48, 216), BF16),
     ]
-    sems = [(6,), (4,), (4,), (4,), (4,), (2, 2, 6), (2, 2, 6), (2,), (2,), (1,), (1,)]
+    sems = [(6,), (4,), (4,), (4,), (4,), (2,), (2, 2, 2), (2,), (2,), (1,), (1,)]
     out_shape = (
         jax.ShapeDtypeStruct((ROWS, D), BF16),
         jax.ShapeDtypeStruct((ROWS, D), BF16),

time: 58.8 us -> 57.1 us (0.971)
  Pallas kernels: 58.1 us -> 56.3 us
    pallas_call x1, Pallas kernels: 56.2 us -> 54.4 us  [shards(): pl.pallas_call(kernel, out_shape=out_shape, in_specs=[hbm] * 4, out_specs...]
where the time goes in v4:
time: 57.1 us; the launch traced here: 57 us
  Pallas kernels  56.3 us (99%)
  between operations  0.64 us (1%)
    pallas_call x1, Pallas kernels, shards(): pl.pallas_call(kernel, out_shape=out_shape, in_specs=[hbm] * 4, out_specs...  54.4 us
    pallas_call x1, Pallas kernels, shards(): pl.pallas_call(hand_over, out_shape=out_shape, in_specs=[vmem] * 4, out_s...  1.9 us

profile of v4, /device:TPU:1, one launch (start us, length us, event | category | flops | bytes accessed | tf_op | source)
XLA Modules:
  0.0 57.0 jit_solution(8266261792058296355)
XLA Ops:
  0.6 54.4 %shard_map.75 = (bf16[128,1152]{1,0:T(8,128)(2,1)}, bf16[128,1152]{1,0:T(8,128)(2,1)}, f32[36,216]{1,0:T(8,128)}, f32[18,144]{1,0:T(8,128)}) custom-call(bf16[128,1152]{1,0:T(8,128)(2,1)} %bitcast.6, bf16[128,1152]{1,0:T(8,128)(2,1)} %bitcast.7, bf16[1728,1152]{1,0:T(8,128)(2,1)} %bitcast.5, bf16[576,1152]{1,0:T(8,128)(2,1)} %wout_hbm.1), custom_call_target="tpu_custom_call" | custom-call | tf_op jit(solution)/shard_map/pallas_call | solution.py:438
  55.1 1.9 %shard_map.76 = (bf16[128,1152]{1,0:T(8,128)(2,1)}, bf16[128,1152]{1,0:T(8,128)(2,1)}, f32[36,216]{1,0:T(8,128)}, f32[18,144]{1,0:T(8,128)}) custom-call(bf16[128,1152]{1,0:T(8,128)(2,1)} %get-tuple-element.12.refs_0_, bf16[128,1152]{1,0:T(8,128)(2,1)} %get-tuple-element.13.refs_1_, f32[36,216]{1,0:T(8,128)} %get-tuple-element.14.refs_2_, ...), custom_call_target="tpu_custom_call" | custom-call | tf_op jit(solution)/shard_map/pallas_call | solution.py:448

commit v5 on v4

--- a/solution.py
+++ b/solution.py
@@ -140,6 +140,15 @@
     query = dot(normed, wqkv[0:HD, :], (1, 1)).astype(BF16)
     key = dot(normed, wqkv[HD : 2 * HD, :], (1, 1)).astype(BF16)
     value = dot(normed, wqkv[2 * HD : 3 * HD, :], (1, 1)).astype(BF16)
+    ntr[...] = xhat[...].T
+    for p in range(PLANE):
+        begin = 144 * (p % 4) + 36 * (p // 4)
+        arr[begin : begin + 36, :] = ntr[36 * p : 36 * p + 36, :]
+    arr[576:, :] = ntr[576:, :]
+    amine[...] = arr[...].astype(BF16)
+    swap_a = remote(amine, apart, c_ss.at[1], c_rs.at[1], mate, seq)
+    swap_a.start()
+
     lane = lax.broadcasted_iota(jnp.int32, (ROWS, HD), 1)
 
     def stack(block, out):
@@ -152,6 +161,7 @@
         return jnp.concatenate([block[h * ROWS : (h + 1) * ROWS, :] for h in range(HEADS)], axis=1)
 
     stack(query, qb)
+    stack(key, kb)
     stack(value, vb)
     scores = dot(qb[...], key, (1, 1)) * SCALE
     here = lax.broadcasted_iota(jnp.int32, (HEADS * ROWS, ROWS), 0)
@@ -165,16 +175,6 @@
     pack(slim, ats)
     push_all(ats, atr, 2)
 
-    ntr[...] = xhat[...].T
-    for p in range(PLANE):
-        begin = 144 * (p % 4) + 36 * (p // 4)
-        arr[begin : begin + 36, :] = ntr[36 * p : 36 * p + 36, :]
-    arr[576:, :] = ntr[576:, :]
-    amine[...] = arr[...].astype(BF16)
-    swap_a = remote(amine, apart, c_ss.at[1], c_rs.at[1], mate, seq)
-    swap_a.start()
-
-    stack(key, kb)
     take_all(gs, gr, 1)
     unpack(gr, slim)
     stack(slim[...], gab)

time: 57.1 us -> 57 us (level)
  no operation moved by 1% of the time
where the time goes in v5:
time: 57 us; the launch traced here: 56.9 us
  Pallas kernels  56.2 us (99%)
  between operations  0.64 us (1%)
    pallas_call x1, Pallas kernels, shards(): pl.pallas_call(kernel, out_shape=out_shape, in_specs=[hbm] * 4, out_specs...  54.4 us
    pallas_call x1, Pallas kernels, shards(): pl.pallas_call(hand_over, out_shape=out_shape, in_specs=[vmem] * 4, out_s...  1.9 us

profile of v5, /device:TPU:1, one launch (start us, length us, event | category | flops | bytes accessed | tf_op | source)
XLA Modules:
  0.0 56.9 jit_solution(12870510444290306893)
XLA Ops:
  0.6 54.4 %shard_map.75 = (bf16[128,1152]{1,0:T(8,128)(2,1)}, bf16[128,1152]{1,0:T(8,128)(2,1)}, f32[36,216]{1,0:T(8,128)}, f32[18,144]{1,0:T(8,128)}) custom-call(bf16[128,1152]{1,0:T(8,128)(2,1)} %bitcast.6, bf16[128,1152]{1,0:T(8,128)(2,1)} %bitcast.7, bf16[1728,1152]{1,0:T(8,128)(2,1)} %bitcast.5, bf16[576,1152]{1,0:T(8,128)(2,1)} %wout_hbm.1), custom_call_target="tpu_custom_call" | custom-call | tf_op jit(solution)/shard_map/pallas_call | solution.py:438
  55.0 1.9 %shard_map.76 = (bf16[128,1152]{1,0:T(8,128)(2,1)}, bf16[128,1152]{1,0:T(8,128)(2,1)}, f32[36,216]{1,0:T(8,128)}, f32[18,144]{1,0:T(8,128)}) custom-call(bf16[128,1152]{1,0:T(8,128)(2,1)} %get-tuple-element.12.refs_0_, bf16[128,1152]{1,0:T(8,128)(2,1)} %get-tuple-element.13.refs_1_, f32[36,216]{1,0:T(8,128)} %get-tuple-element.14.refs_2_, ...), custom_call_target="tpu_custom_call" | custom-call | tf_op jit(solution)/shard_map/pallas_call | solution.py:448

commit v6 on v5

--- a/solution.py
+++ b/solution.py
@@ -28,13 +28,13 @@
 
 def kernel(
     tok_hbm, cot_hbm, wqkv_hbm, wout_hbm,
-    result_hbm, gtok_hbm, gwq, gwo,
+    result_hbm, gtok_hbm, zrecv,
     tok, cot, wqkv, wout, result, gtok,
     wide, slim, xhat, cotp,
     xs, xr, gs, gr, ats, atr, gbs, gbr,
     cots, cotr, ntr, arr, amine, apart, gph, gpart, ttr, tarr, tmine, tpart,
     qb, kb, vb, gab, probs, plow,
-    fsend0, frelay0, fback0, own0, fsend1, frelay1, fback1, own1, hsend, hrecv, zsend, zrecv,
+    fsend0, frelay0, fback0, own0, fsend1, frelay1, fback1, own1, hsend, hrecv, zsend,
     wsem, a_ss, a_rs, c_ss, c_rs, f_ss, f_rs, h_ss, h_rs, z_ss, z_rs,
 ):
     dp, seq = lax.axis_index("dp"), lax.axis_index("seq")
@@ -185,12 +185,11 @@
     grad_query = dot(side(grad_scores), kb[...], (1, 0))
     grad_key = dot(grad_scores, qb[...], (0, 0))
     grad_value = dot(plow[...], gab[...], (0, 0))
-    grad_proj = jnp.concatenate([grad_query, grad_key, grad_value], axis=1)
-    gph[0] = grad_proj[:, :864].astype(BF16)
-    gph[1] = grad_proj[:, 864:].astype(BF16)
+    grad_proj = jnp.concatenate([g.astype(BF16) for g in (grad_query, grad_key, grad_value)], axis=1)
+    gph[0] = grad_proj[:, :864]
+    gph[1] = grad_proj[:, 864:]
     swap_g = remote(gph.at[1 - core], gpart, c_ss.at[2], c_rs.at[2], mate, seq)
     swap_g.start()
-    grad_proj = grad_proj.astype(BF16)
 
     grad_normed = dot(grad_proj, wqkv[...], (1, 0))
     x_hat = xhat[...]
@@ -314,10 +313,6 @@
 
     def gathered():
         pltpu.make_async_copy(zsend, zrecv, z_rs.at[0]).wait()
-        total = zrecv[0].astype(F32)
-        for n in range(1, 8):
-            total = total + zrecv[n].astype(F32)
-        return total * FACTOR
 
     def z_sent(count):
         many = pl.ds(0, count)
@@ -393,18 +388,22 @@
     store_gtok = pltpu.make_async_copy(gtok, gtok_hbm, wsem.at[5])
     store_gtok.start()
     sent_all(gbs, gbr, 3)
-    owned = gathered()
+    gathered()
+    all_sent()
+    store_result.wait()
+    store_gtok.wait()
+
+
+def hand_over(result, gtok, pieces, result_out, gtok_out, gwq, gwo):
+    result_out[...] = result[...]
+    gtok_out[...] = gtok[...]
+    total = pieces[0].astype(F32)
+    for n in range(1, 8):
+        total = total + pieces[n].astype(F32)
+    owned = total * FACTOR
     gwq[...] = owned[:36, :]
     gwo[0:12, :] = owned[36:48, 0:144]
     gwo[12:18, :] = jnp.concatenate([owned[36:42, 144:216], owned[42:48, 144:216]], axis=1)
-    all_sent()
-    store_result.wait()
-    store_gtok.wait()
-
-
-def hand_over(*refs):
-    for n in range(4):
-        refs[4 + n][...] = refs[n][...]
 
 
 def shards(tokens, cotangent, w_qkv, w_out):
@@ -426,7 +425,7 @@
         ((HEADS * ROWS, ROWS), F32), ((HEADS * ROWS, ROWS), BF16),
         ((2, 3, 144, 864), BF16), ((2, 144, 864), BF16), ((2, 2, 144, 864), BF16), ((2, 144, 864), F32),
         ((2, 3, 48, 864), BF16), ((2, 48, 864), BF16), ((2, 2, 48, 864), BF16), ((2, 48, 864), F32),
-        ((2, 4, 48, 864), BF16), ((2, 4, 48, 864), BF16), ((8, 48, 216), BF16), ((8, 48, 216), BF16),
+        ((2, 4, 48, 864), BF16), ((2, 4, 48, 864), BF16), ((8, 48, 216), BF16),
     ]
     sems = [(6,), (4,), (4,), (4,), (4,), (2,), (2, 2, 2), (2,), (2,), (1,), (1,)]
     out_shape = (
@@ -437,9 +436,9 @@
     )
     outs = pl.pallas_call(
         kernel,
-        out_shape=out_shape,
+        out_shape=out_shape[:2] + (jax.ShapeDtypeStruct((8, 48, 216), BF16),),
         in_specs=[hbm] * 4,
-        out_specs=(hbm, hbm, vmem, vmem),
+        out_specs=(hbm,) * 3,
         scratch_shapes=[pltpu.VMEM(s, t) for s, t in scratch] + [dma(n) for n in sems],
         compiler_params=pltpu.CompilerParams(
             collective_id=0, has_side_effects=True, vmem_limit_bytes=56 * 1024 * 1024
@@ -448,7 +447,7 @@
     result, gtok, gwq, gwo = pl.pallas_call(
         hand_over,
         out_shape=out_shape,
-        in_specs=[vmem] * 4,
+        in_specs=[vmem] * 3,
         out_specs=(vmem,) * 4,
     )(*outs)
     return (result.reshape(shape), gtok.reshape(shape), gwq, gwo)

time: 57 us -> 56.5 us (level)
  no operation moved by 1% of the time
where the time goes in v6:
time: 56.5 us; the launch traced here: 56.4 us
  Pallas kernels  55.7 us (99%)
  between operations  0.64 us (1%)
    pallas_call x1, Pallas kernels, shards(): pl.pallas_call(kernel, out_shape=out_shape[:2] + (jax.ShapeDtypeStruct((8...  53.8 us
    pallas_call x1, Pallas kernels, shards(): pl.pallas_call(hand_over, out_shape=out_shape, in_specs=[vmem] * 3, out_s...  1.97 us

profile of v6, /device:TPU:1, one launch (start us, length us, event | category | flops | bytes accessed | tf_op | source)
XLA Modules:
  0.0 56.4 jit_solution(18257266184666462101)
XLA Ops:
  0.6 53.8 %shard_map.75 = (bf16[128,1152]{1,0:T(8,128)(2,1)}, bf16[128,1152]{1,0:T(8,128)(2,1)}, bf16[8,48,216]{2,1,0:T(8,128)(2,1)}) custom-call(bf16[128,1152]{1,0:T(8,128)(2,1)} %bitcast.6, bf16[128,1152]{1,0:T(8,128)(2,1)} %bitcast.7, bf16[1728,1152]{1,0:T(8,128)(2,1)} %bitcast.5, bf16[576,1152]{1,0:T(8,128)(2,1)} %wout_hbm.1), custom_call_target="tpu_custom_call" | custom-call | tf_op jit(solution)/shard_map/pallas_call | solution.py:437
  54.4 2.0 %shard_map.76 = (bf16[128,1152]{1,0:T(8,128)(2,1)}, bf16[128,1152]{1,0:T(8,128)(2,1)}, f32[36,216]{1,0:T(8,128)}, f32[18,144]{1,0:T(8,128)}) custom-call(bf16[128,1152]{1,0:T(8,128)(2,1)} %get-tuple-element.11.result, bf16[128,1152]{1,0:T(8,128)(2,1)} %get-tuple-element.12.gtok, bf16[8,48,216]{2,1,0:T(8,128)(2,1)} %get-tuple-element.13.pieces), custom_call_target="tpu_custom_call" | custom-call | tf_op jit(solution)/shard_map/pallas_call | solution.py:447

commit v7 on v6

--- a/solution.py
+++ b/solution.py
@@ -201,10 +201,6 @@
     def push_rows(to):
         remote(gbs.at[to], gbr.at[seq], a_ss.at[3], a_rs.at[3], dp, to).start()
 
-    @pl.loop(0, PLANE)
-    def _(k):
-        push_rows((1 - z_lo) * PLANE + (xy + k) % PLANE)
-
     swap_a.wait_recv()
     swap_g.wait_recv()
 
@@ -351,6 +347,11 @@
     swap_t.start()
     near(0)
     near_push(0)
+
+    @pl.loop(0, PLANE)
+    def _(k):
+        push_rows((1 - z_lo) * PLANE + (xy + k) % PLANE)
+
     swap_cot.wait_recv()
     swap_t.wait_recv()
     opposite(1)

time: 56.5 us -> 57.3 us (1.014)
  Pallas kernels: 55.7 us -> 56.6 us
    pallas_call x1, Pallas kernels: 53.8 us -> 54.6 us  [shards(): pl.pallas_call(kernel, out_shape=out_shape[:2] + (jax.ShapeDtypeStruct((8...]
where the time goes in v7:
time: 57.3 us; the launch traced here: 57.2 us
  Pallas kernels  56.6 us (99%)
  between operations  0.64 us (1%)
    pallas_call x1, Pallas kernels, shards(): pl.pallas_call(kernel, out_shape=out_shape[:2] + (jax.ShapeDtypeStruct((8...  54.6 us
    pallas_call x1, Pallas kernels, shards(): pl.pallas_call(hand_over, out_shape=out_shape, in_specs=[vmem] * 3, out_s...  1.97 us

profile of v7, /device:TPU:1, one launch (start us, length us, event | category | flops | bytes accessed | tf_op | source)
XLA Modules:
  0.0 57.2 jit_solution(4103108155044595134)
XLA Ops:
  0.6 54.6 %shard_map.75 = (bf16[128,1152]{1,0:T(8,128)(2,1)}, bf16[128,1152]{1,0:T(8,128)(2,1)}, bf16[8,48,216]{2,1,0:T(8,128)(2,1)}) custom-call(bf16[128,1152]{1,0:T(8,128)(2,1)} %bitcast.6, bf16[128,1152]{1,0:T(8,128)(2,1)} %bitcast.7, bf16[1728,1152]{1,0:T(8,128)(2,1)} %bitcast.5, bf16[576,1152]{1,0:T(8,128)(2,1)} %wout_hbm.1), custom_call_target="tpu_custom_call" | custom-call | tf_op jit(solution)/shard_map/pallas_call | solution.py:438
  55.2 2.0 %shard_map.76 = (bf16[128,1152]{1,0:T(8,128)(2,1)}, bf16[128,1152]{1,0:T(8,128)(2,1)}, f32[36,216]{1,0:T(8,128)}, f32[18,144]{1,0:T(8,128)}) custom-call(bf16[128,1152]{1,0:T(8,128)(2,1)} %get-tuple-element.11.result, bf16[128,1152]{1,0:T(8,128)(2,1)} %get-tuple-element.12.gtok, bf16[8,48,216]{2,1,0:T(8,128)(2,1)} %get-tuple-element.13.pieces), custom_call_target="tpu_custom_call" | custom-call | tf_op jit(solution)/shard_map/pallas_call | solution.py:448

commit v8 on v6

--- a/solution.py
+++ b/solution.py
@@ -298,18 +298,19 @@
             for j in range(4):
                 zsend[2 * j + t] = total[:, 216 * j : 216 * j + 216].astype(BF16)
 
-        @pl.loop(0, 8)
-        def _(n):
-            to_dp, to_seq = z_target(n)
-            is_me = (to_dp == dp) & (to_seq == seq)
-
-            @pl.when(is_me)
-            def _():
-                pltpu.make_async_copy(zsend.at[n], zrecv.at[zed], z_rs.at[0]).start()
-
-            @pl.when(jnp.logical_not(is_me))
-            def _():
-                remote(zsend.at[n], zrecv.at[zed], z_ss.at[0], z_rs.at[0], to_dp, to_seq).start()
+            @pl.loop(0, 4)
+            def _(j):
+                n = 2 * j + t
+                to_dp, to_seq = z_target(n)
+                is_me = (to_dp == dp) & (to_seq == seq)
+
+                @pl.when(is_me)
+                def _():
+                    pltpu.make_async_copy(zsend.at[n], zrecv.at[zed], z_rs.at[0]).start()
+
+                @pl.when(jnp.logical_not(is_me))
+                def _():
+                    remote(zsend.at[n], zrecv.at[zed], z_ss.at[0], z_rs.at[0], to_dp, to_seq).start()
 
     def gathered():
         pltpu.make_async_copy(zsend, zrecv, z_rs.at[0]).wait()

time: 56.5 us -> 57.4 us (1.016)
  Pallas kernels: 55.7 us -> 56.7 us
    pallas_call x1, Pallas kernels: 53.8 us -> 54.7 us  [shards(): pl.pallas_call(kernel, out_shape=out_shape[:2] + (jax.ShapeDtypeStruct((8...]
where the time goes in v8:
time: 57.4 us; the launch traced here: 57.3 us
  Pallas kernels  56.7 us (99%)
  between operations  0.64 us (1%)
    pallas_call x1, Pallas kernels, shards(): pl.pallas_call(kernel, out_shape=out_shape[:2] + (jax.ShapeDtypeStruct((8...  54.7 us
    pallas_call x1, Pallas kernels, shards(): pl.pallas_call(hand_over, out_shape=out_shape, in_specs=[vmem] * 3, out_s...  1.97 us

profile of v8, /device:TPU:1, one launch (start us, length us, event | category | flops | bytes accessed | tf_op | source)
XLA Modules:
  0.0 57.3 jit_solution(14176688122740536172)
XLA Ops:
  0.6 54.7 %shard_map.75 = (bf16[128,1152]{1,0:T(8,128)(2,1)}, bf16[128,1152]{1,0:T(8,128)(2,1)}, bf16[8,48,216]{2,1,0:T(8,128)(2,1)}) custom-call(bf16[128,1152]{1,0:T(8,128)(2,1)} %bitcast.6, bf16[128,1152]{1,0:T(8,128)(2,1)} %bitcast.7, bf16[1728,1152]{1,0:T(8,128)(2,1)} %bitcast.5, bf16[576,1152]{1,0:T(8,128)(2,1)} %wout_hbm.1), custom_call_target="tpu_custom_call" | custom-call | tf_op jit(solution)/shard_map/pallas_call | solution.py:438
  55.3 2.0 %shard_map.76 = (bf16[128,1152]{1,0:T(8,128)(2,1)}, bf16[128,1152]{1,0:T(8,128)(2,1)}, f32[36,216]{1,0:T(8,128)}, f32[18,144]{1,0:T(8,128)}) custom-call(bf16[128,1152]{1,0:T(8,128)(2,1)} %get-tuple-element.11.result, bf16[128,1152]{1,0:T(8,128)(2,1)} %get-tuple-element.12.gtok, bf16[8,48,216]{2,1,0:T(8,128)(2,1)} %get-tuple-element.13.pieces), custom_call_target="tpu_custom_call" | custom-call | tf_op jit(solution)/shard_map/pallas_call | solution.py:448
